TPU v7x, 32 devices: a whole 2x2x4 slice. The times are simulated.
32 devices in a mesh: ctx: 8 (over z, x), tp: 4 (over y, core).
Axes of the slice: x: 2, y: 2, z: 4, core: 2. Of those that a mesh axis runs over, the one named last changes fastest.
Arguments:
- query_in: bfloat16 [2048, 1024], P('tp', 'ctx'), may hold values from -6 to 6
- key_in: bfloat16 [2048, 1024], P('tp', 'ctx'), may hold values from -6 to 6
- value_in: bfloat16 [2048, 1024], P('tp', 'ctx'), may hold values from -6 to 6
- short_weights: float32 [3, 2048, 7], P(None, 'tp'), may hold values from -3 to 3
- filters: float32 [4, 512, 1024], P('tp', 'ctx'), may hold values from 0 to 1
- out_weight: bfloat16 [4096, 2048], P(None, 'tp'), may hold values from -0.125 to 0.125
- cotangent: bfloat16 [4096, 1024], P('tp', 'ctx'), may hold values from -6 to 6
Outputs:
- mixed_out: bfloat16 [4096, 1024], P('tp', 'ctx')
- grad_query: bfloat16 [2048, 1024], P('tp', 'ctx')
- grad_key: bfloat16 [2048, 1024], P('tp', 'ctx')
- grad_value: bfloat16 [2048, 1024], P('tp', 'ctx')
- grad_filters: float32 [4, 512, 1024], P('tp', 'ctx')
- grad_out_weight: float32 [4096, 2048], P('ctx', 'tp')
All inputs are finite; a program needn't handle non-finite values.
Results may differ from a plain program's by a relative error of at most 0.012.
Values may be sent and summed in bfloat16 or wider, within the bound.
A program may use at most 128 MiB of HBM per device.

v0:
```python
import math

import jax
import jax.numpy as jnp
from jax import lax
from jax.sharding import PartitionSpec as P

BLOCK = 128


TWO_PI = 2.0 * math.pi
HIGHEST = lax.Precision.HIGHEST


def from_behind(value, axis, steps):
    count = lax.axis_size(axis)
    first, last = (max(0, -steps), min(count, count - steps))
    return lax.ppermute(value, axis, [(source, source + steps) for source in range(first, last)])


def fourier_table(count):
    element_indices = jnp.arange(count, dtype=jnp.int32)
    angles = (element_indices[:, None] * element_indices[None, :] % count).astype(jnp.float32) * (
        TWO_PI / count
    )
    return (jnp.cos(angles), -jnp.sin(angles))


def make_tables(length, block_width):
    row_count = 2 * length // block_width
    full_len = row_count * block_width
    outer_re, outer_im = fourier_table(row_count)
    inner_re, inner_im = fourier_table(block_width)
    row_index = jnp.arange(row_count, dtype=jnp.int32)[:, None]
    col_index = jnp.arange(block_width, dtype=jnp.int32)[None, :]
    angles = (row_index * col_index % full_len).astype(jnp.float32) * (TWO_PI / full_len)
    return (outer_re, outer_im, inner_re, inner_im, jnp.cos(angles), -jnp.sin(angles))


def spectrum(signal, tables):
    outer_re, outer_im, inner_re, inner_im, twist_re, twist_im = tables
    channels, length = signal.shape
    block_width = inner_re.shape[0]
    half_rows = length // block_width
    blocks = signal.reshape(channels, half_rows, block_width)
    section_re = jnp.einsum("kn,cnm->ckm", outer_re[:, :half_rows], blocks, precision=HIGHEST)
    section_im = jnp.einsum("kn,cnm->ckm", outer_im[:, :half_rows], blocks, precision=HIGHEST)
    turned_re = section_re * twist_re - section_im * twist_im
    turned_im = section_re * twist_im + section_im * twist_re
    frequency_real_component = jnp.matmul(turned_re, inner_re, precision=HIGHEST) - jnp.matmul(
        turned_im, inner_im, precision=HIGHEST
    )
    spec_im = jnp.matmul(turned_re, inner_im, precision=HIGHEST) + jnp.matmul(
        turned_im, inner_re, precision=HIGHEST
    )
    return (frequency_real_component, spec_im)


def inverse(frequency_real_component, spec_im, tables):
    outer_re, outer_im, inner_re, inner_im, twist_re, twist_im = tables
    channels, row_count, block_width = frequency_real_component.shape
    half_rows = row_count // 2
    back_re = jnp.matmul(frequency_real_component, inner_re, precision=HIGHEST) + jnp.matmul(
        spec_im, inner_im, precision=HIGHEST
    )
    back_im = jnp.matmul(spec_im, inner_re, precision=HIGHEST) - jnp.matmul(
        frequency_real_component, inner_im, precision=HIGHEST
    )
    turned_re = back_re * twist_re + back_im * twist_im
    turned_im = back_im * twist_re - back_re * twist_im
    signal = jnp.einsum("nk,ckm->cnm", outer_re[:half_rows], turned_re, precision=HIGHEST)
    signal = signal + jnp.einsum("nk,ckm->cnm", outer_im[:half_rows], turned_im, precision=HIGHEST)
    return (signal / (row_count * block_width)).reshape(channels, half_rows * block_width)


def causal_taps(stacked, earlier, weights):
    tap_count = weights.shape[2]
    length = stacked.shape[2]
    extended = jnp.concatenate([earlier, stacked], axis=2).astype(jnp.float32)
    running_total = jnp.zeros(stacked.shape, jnp.float32)
    for offset in range(tap_count):
        begin = tap_count - 1 - offset
        running_total = (
            running_total
            + weights[:, :, offset : offset + 1] * extended[:, :, begin : begin + length]
        )
    return running_total


def anticausal_taps(stacked, following, weights):
    tap_count = weights.shape[2]
    length = stacked.shape[2]
    extended = jnp.concatenate([stacked, following], axis=2).astype(jnp.float32)
    running_total = jnp.zeros(stacked.shape, jnp.float32)
    for offset in range(tap_count):
        running_total = (
            running_total
            + weights[:, :, offset : offset + 1] * extended[:, :, offset : offset + length]
        )
    return running_total


def to_channels(block):
    return lax.all_to_all(block, "ctx", split_axis=0, concat_axis=1, tiled=True)


def to_positions(block):
    return lax.all_to_all(block, "ctx", split_axis=1, concat_axis=0, tiled=True)


def per_device(query_in, key_in, value_in, short_weights, filters, out_weight, cotangent):
    tap_count = short_weights.shape[2]
    local_len = query_in.shape[1]
    stacked = jnp.stack([query_in, key_in, value_in])
    earlier = from_behind(stacked[:, :, local_len - (tap_count - 1) :], "ctx", 1)
    shorts = causal_taps(stacked, earlier, short_weights).astype(jnp.bfloat16)
    product = (shorts[1].astype(jnp.float32) * shorts[2].astype(jnp.float32)).astype(jnp.bfloat16)
    product_chan = to_channels(product)
    tables = make_tables(product_chan.shape[1], BLOCK)
    kernel_re, kernel_im = spectrum(filters[0], tables)
    product_re, product_im = spectrum(product_chan.astype(jnp.float32), tables)
    convolved_chan = inverse(
        product_re * kernel_re - product_im * kernel_im,
        product_re * kernel_im + product_im * kernel_re,
        tables,
    ).astype(jnp.bfloat16)
    convolved = to_positions(convolved_chan)
    gated_out = (shorts[0].astype(jnp.float32) * convolved.astype(jnp.float32)).astype(jnp.bfloat16)
    mixed_out = lax.psum_scatter(
        jnp.dot(out_weight, gated_out, preferred_element_type=jnp.float32).astype(jnp.bfloat16),
        "tp",
        scatter_dimension=0,
        tiled=True,
    )
    full_cotangent = lax.all_gather(cotangent, "tp", axis=0, tiled=True)
    grad_gated = lax.dot_general(
        out_weight, full_cotangent, (((0,), (0,)), ((), ())), preferred_element_type=jnp.float32
    )
    grad_out_weight = lax.psum_scatter(
        lax.dot_general(
            full_cotangent, gated_out, (((1,), (1,)), ((), ())), preferred_element_type=jnp.float32
        ),
        "ctx",
        scatter_dimension=0,
        tiled=True,
    )
    grad_conv = (grad_gated * shorts[0].astype(jnp.float32)).astype(jnp.bfloat16)
    grad_chan = to_channels(grad_conv)
    gradient_re, gradient_im = spectrum(grad_chan.astype(jnp.float32), tables)
    grad_product_chan = inverse(
        kernel_re * gradient_re + kernel_im * gradient_im,
        kernel_re * gradient_im - kernel_im * gradient_re,
        tables,
    ).astype(jnp.bfloat16)
    grad_filters = inverse(
        product_re * gradient_re + product_im * gradient_im,
        product_re * gradient_im - product_im * gradient_re,
        tables,
    ).reshape(filters.shape)
    derivative_of_multiple = to_positions(grad_product_chan)
    grad_shorts = jnp.stack(
        [
            grad_gated * convolved.astype(jnp.float32),
            derivative_of_multiple.astype(jnp.float32) * shorts[2].astype(jnp.float32),
            derivative_of_multiple.astype(jnp.float32) * shorts[1].astype(jnp.float32),
        ]
    ).astype(jnp.bfloat16)
    following = from_behind(grad_shorts[:, :, : tap_count - 1], "ctx", -1)
    gradients = anticausal_taps(grad_shorts, following, short_weights).astype(jnp.bfloat16)
    return (mixed_out, gradients[0], gradients[1], gradients[2], grad_filters, grad_out_weight)


def solution(mesh):
    placed = (
        P("tp", "ctx"),
        P("tp", "ctx"),
        P("tp", "ctx"),
        P(None, "tp", None),
        P("tp", "ctx", None),
        P(None, "tp"),
        P("tp", "ctx"),
    )
    return jax.shard_map(
        per_device,
        mesh=mesh,
        in_specs=placed,
        out_specs=(
            P("tp", "ctx"),
            P("tp", "ctx"),
            P("tp", "ctx"),
            P("tp", "ctx"),
            P("tp", "ctx", None),
            P("ctx", "tp"),
        ),
        check_vma=False,
    )
```

profile of v0, /device:TPU:0, one launch (start us, length us, event | category | flops | bytes accessed | tf_op | source)
XLA Modules:
  0.0 263.9 jit_solution(5199044125280835380)
XLA Ops:
  7.2 0.7 all-gather.2.cloned.1.call-update
  7.9 1.0 copy.52
  8.9 1.0 copy.53
  9.9 1.0 copy.54
  11.0 4.8 %collective-permute-start = (bf16[3,512,6]{1,2,0:T(8,128)(2,1)S(1)}, bf16[3,512,6]{1,2,0:T(8,128)(2,1)S(1)}, u32[]{:S(2)}, u32[]{:S(2)}) collective-permute-start(bf16[3,512,6]{1,2,0:T(8,128)(2,1)S(1)} %pad_maximum_fusion.2), channel_id=1, source_target_pairs={{0,4},{4,8},{8,12},{12,16},{16,20},{20,24},{24,28},{1,5},{5,9},{9,... | collective-permute-start | bytes 55304 | tf_op jit(solution)/shard_map/ppermute | solution.py:18
  16.0 1.0 copy.95
  17.0 0.6 fusion.144
  17.6 0.6 fusion.143
  18.3 0.8 fusion.25
  19.1 0.8 fusion.27
  20.0 1.6 convolution_add_fusion.4
  21.8 0.7 fusion.17
  22.5 0.8 copy.55
  23.3 4.9 %all-to-all-start = ((bf16[8,64,128]{2,1,0:T(8,128)(2,1)}), bf16[8,64,128]{2,1,0:T(8,128)(2,1)S(1)}, u32[]{:S(2)}, u32[]{:S(2)}) async-start(bf16[8,64,128]{2,1,0:T(8,128)(2,1)} %bitcast.4), calls=%async_computation | async-start | bytes 262144 | tf_op jit(solution)/shard_map/all_to_all | solution.py:104
  28.2 1.6 convolution_subtract_fusion.4
  29.8 5.7 %all-to-all-done = bf16[8,64,128]{2,1,0:T(8,128)(2,1)S(1)} async-done(((bf16[8,64,128]{2,1,0:T(8,128)(2,1)}), bf16[8,64,128]{2,1,0:T(8,128)(2,1)S(1)}, u32[]{:S(2)}, u32[]{:S(2)}) %all-to-all-start) | async-done | bytes 131104 | tf_op jit(solution)/shard_map/all_to_all | solution.py:104
  36.4 0.8 fusion.68
  37.2 1.6 convolution_subtract_fusion.5
  38.8 4.0 %fusion.54 = (bf16[512,128]{0,1:T(8,128)(2,1)S(1)}, f32[512,128]{0,1:T(8,128)}) fusion(bf16[3,512,128]{1,2,0:T(8,128)(2,1)S(1)} %fusion.17, bf16[4096,512]{1,0:T(8,128)(2,1)} %param.12, bf16[4096,128]{1,0:T(8,128)(2,1)} %all-gather.2.cloned.1.call-done), kind=kOutput, calls=%fused_computation.108 | convolution fusion | flops 537067520 | bytes 5767168 | tf_op jit(solution)/shard_map/dot_general | solution.py:136
  42.8 0.8 copy.62
  43.6 3.4 %all-to-all-start.2 = ((bf16[8,64,128]{2,1,0:T(8,128)(2,1)}), bf16[8,64,128]{2,1,0:T(8,128)(2,1)S(1)}, u32[]{:S(2)}, u32[]{:S(2)}) async-start(bf16[8,64,128]{2,1,0:T(8,128)(2,1)} %bitcast.23), calls=%async_computation.3 | async-start | bytes 262144 | tf_op jit(solution)/shard_map/all_to_all | solution.py:104
  47.2 1.6 fusion.67
  48.8 5.4 %all-to-all-done.2 = bf16[8,64,128]{2,1,0:T(8,128)(2,1)S(1)} async-done(((bf16[8,64,128]{2,1,0:T(8,128)(2,1)}), bf16[8,64,128]{2,1,0:T(8,128)(2,1)S(1)}, u32[]{:S(2)}, u32[]{:S(2)}) %all-to-all-start.2) | async-done | bytes 131104 | tf_op jit(solution)/shard_map/all_to_all | solution.py:104
  54.7 0.4 convolution_bitcast_fusion.2
  55.1 0.8 fusion.69
  55.9 0.8 fusion.70
  56.8 0.8 convolution_add_fusion.2
  57.6 0.8 convolution_subtract_fusion.2
  58.5 1.1 multiply_add_fusion
  59.6 0.8 fusion.105
  60.4 0.8 fusion.107
  61.2 0.8 convolution_subtract_fusion.3
  62.1 0.8 convolution_add_fusion.3
  62.9 0.5 fusion.46
  63.4 0.5 fusion.8
  63.9 9.7 %all_to_all.49 = bf16[64,8,128]{2,0,1:T(8,128)(2,1)S(1)} all-to-all(bf16[64,8,128]{2,0,1:T(8,128)(2,1)S(1)} %copy.59), channel_id=1, replica_groups=mesh['ctx'=8,'tp'=4] {'ctx'}, dimensions={1} | all-to-all | bytes 262144 | tf_op jit(solution)/shard_map/all_to_all | solution.py:108
  73.8 4.6 %fusion = bf16[4096,128]{0,1:T(8,128)(2,1)} fusion(bf16[4096,512]{1,0:T(8,128)(2,1)} %param.12, f32[512,128]{0,1:T(8,128)S(1)} %copy.60, bf16[3,512,128]{1,2,0:T(8,128)(2,1)S(1)} %copy-done.1), kind=kOutput, calls=%fused_computation.2 | convolution fusion | flops 537591808 | bytes 5636096 | tf_op jit(solution)/shard_map/dot_general | solution.py:130
  78.7 5.8 %convolution_bitcast_fusion = f32[4096,512]{0,1:T(8,128)} fusion(bf16[4096,128]{1,0:T(8,128)(2,1)} %all-gather.2.cloned.1.call-done, f32[512,128]{0,1:T(8,128)S(1)} %copy.60, bf16[3,512,128]{1,2,0:T(8,128)(2,1)S(1)} %copy-done.1), kind=kOutput, calls=%fused_computation | convolution fusion | flops 537067520 | bytes 9830400 | tf_op jit(solution)/shard_map/dot_general | solution.py:140
  84.5 0.8 fusion.99
  85.3 0.8 fusion.101
  86.2 0.8 convolution_subtract_fusion.1
  87.0 0.8 convolution_add_fusion.1
  87.8 0.5 fusion.39
  88.3 0.5 fusion.7
  88.8 0.7 copy.66
  89.4 3.4 %all-to-all-start.3 = ((bf16[64,8,128]{2,0,1:T(8,128)(2,1)}), bf16[64,8,128]{2,0,1:T(8,128)(2,1)S(1)}, u32[]{:S(2)}, u32[]{:S(2)}) async-start(bf16[64,8,128]{2,0,1:T(8,128)(2,1)} %copy.66), calls=%async_computation.4 | async-start | bytes 262144 | tf_op jit(solution)/shard_map/all_to_all | solution.py:108
  92.8 0.8 fusion.97
  93.6 0.8 fusion.95
  94.5 0.8 convolution_add_fusion
  95.3 0.8 convolution_subtract_fusion
  96.1 0.5 fusion.32
  96.6 3.5 %all-to-all-done.3 = bf16[64,8,128]{2,0,1:T(8,128)(2,1)S(1)} async-done(((bf16[64,8,128]{2,0,1:T(8,128)(2,1)}), bf16[64,8,128]{2,0,1:T(8,128)(2,1)S(1)}, u32[]{:S(2)}, u32[]{:S(2)}) %all-to-all-start.3) | async-done | bytes 131104 | tf_op jit(solution)/shard_map/all_to_all | solution.py:108
  100.3 1.0 fusion.71
  101.3 1.3 collective-permute-start.1
  102.6 0.5 fusion.2
  103.1 0.7 reshape_reshape.3
  103.8 3.2 %collective-permute-done.1 = bf16[3,512,6]{1,2,0:T(8,128)(2,1)S(1)} collective-permute-done((bf16[3,512,6]{1,2,0:T(8,128)(2,1)S(1)}, bf16[3,512,6]{1,2,0:T(8,128)(2,1)S(1)}, u32[]{:S(2)}, u32[]{:S(2)}) %collective-permute-start.1) | collective-permute-done | bytes 18464 | tf_op jit(solution)/shard_map/ppermute | solution.py:18
  107.1 0.7 fusion.10
  107.8 0.8 copy.74
  108.6 0.8 copy.73
  109.4 0.8 copy.72
  110.1 1.8 copy.71
  111.9 142.9 %reduce-scatter.5.cloned.1.call-done = f32[512,512]{0,1:T(8,128)} async-done(((f32[4096,512]{0,1:T(8,128)}), f32[512,512]{0,1:T(8,128)}) %reduce-scatter.5.cloned.1.call-update) | async-done | bytes 1048592 | tf_op jit(solution)/shard_map/reduce_scatter | solution.py:139
  254.8 2.5 copy.75
  (45 shorter events, 2.7 us)
Async XLA Ops:
  7.2 12.8 %copy-start.6 = (f32[3,512,7]{1,2,0:T(8,128)S(1)}, f32[3,512,7]{1,2,0:T(8,128)}, u32[]{:S(2)}) copy-start(f32[3,512,7]{1,2,0:T(8,128)} %param.10) | copy-start | bytes 129028
  7.2 31.6 %all-gather.2.cloned.1.call-start = ((), (), s32[]{:S(2)}) async-start(), calls=%async_computation.7 | async-start | bytes 1310720 | tf_op jit(solution)/shard_map/all_gather | solution.py:135
  11.0 10.7 %collective-permute-start = (bf16[3,512,6]{1,2,0:T(8,128)(2,1)S(1)}, bf16[3,512,6]{1,2,0:T(8,128)(2,1)S(1)}, u32[]{:S(2)}, u32[]{:S(2)}) collective-permute-start(bf16[3,512,6]{1,2,0:T(8,128)(2,1)S(1)} %pad_maximum_fusion.2), channel_id=1, source_target_pairs={{0,4},{4,8},{8,12},{12,16},{16,20},{20,24},{24,28},{1,5},{5,9},{9,... | collective-permute-start | bytes 55304 | tf_op jit(solution)/shard_map/ppermute | solution.py:18
  22.5 20.3 %copy-start = (bf16[3,512,128]{1,2,0:T(8,128)(2,1)}, bf16[3,512,128]{1,2,0:T(8,128)(2,1)S(1)}, u32[]{:S(2)}) copy-start(bf16[3,512,128]{1,2,0:T(8,128)(2,1)S(1)} %fusion.17) | copy-start | bytes 1179652
  23.3 12.2 %all-to-all-start = ((bf16[8,64,128]{2,1,0:T(8,128)(2,1)}), bf16[8,64,128]{2,1,0:T(8,128)(2,1)S(1)}, u32[]{:S(2)}, u32[]{:S(2)}) async-start(bf16[8,64,128]{2,1,0:T(8,128)(2,1)} %bitcast.4), calls=%async_computation | async-start | bytes 262144 | tf_op jit(solution)/shard_map/all_to_all | solution.py:104
  43.6 10.7 %all-to-all-start.2 = ((bf16[8,64,128]{2,1,0:T(8,128)(2,1)}), bf16[8,64,128]{2,1,0:T(8,128)(2,1)S(1)}, u32[]{:S(2)}, u32[]{:S(2)}) async-start(bf16[8,64,128]{2,1,0:T(8,128)(2,1)} %bitcast.23), calls=%async_computation.3 | async-start | bytes 262144 | tf_op jit(solution)/shard_map/all_to_all | solution.py:104
  46.9 63.2 %reduce-scatter.3.cloned.1.call-start = ((), (), s32[]{:S(2)}) async-start(), calls=%async_computation.6 | async-start | bytes 1310720 | tf_op jit(solution)/shard_map/reduce_scatter | solution.py:129
  54.6 3.8 %copy-start.2 = (f32[64,16,128]{2,1,0:T(8,128)S(1)}, f32[64,16,128]{2,1,0:T(8,128)}, u32[]{:S(2)}) copy-start(f32[64,16,128]{2,1,0:T(8,128)} %fusion.67) | copy-start | bytes 1572868
  54.7 3.8 %copy-start.3 = (f32[64,16,128]{2,1,0:T(8,128)S(1)}, f32[64,16,128]{2,1,0:T(8,128)}, u32[]{:S(2)}) copy-start(f32[64,16,128]{2,1,0:T(8,128)} %convolution_add_fusion.4) | copy-start | bytes 1572868
  54.7 3.8 %copy-start.4 = (f32[64,16,128]{2,1,0:T(8,128)S(1)}, f32[64,16,128]{2,1,0:T(8,128)}, u32[]{:S(2)}) copy-start(f32[64,16,128]{2,1,0:T(8,128)} %convolution_subtract_fusion.4) | copy-start | bytes 1572868
  54.7 3.8 %copy-start.5 = (f32[64,16,128]{2,1,0:T(8,128)S(1)}, f32[64,16,128]{2,1,0:T(8,128)}, u32[]{:S(2)}) copy-start(f32[64,16,128]{2,1,0:T(8,128)} %convolution_subtract_fusion.5) | copy-start | bytes 1572868
  60.4 13.4 %copy-start.1 = (bf16[3,512,128]{1,2,0:T(8,128)(2,1)S(1)}, bf16[3,512,128]{1,2,0:T(8,128)(2,1)}, u32[]{:S(2)}) copy-start(bf16[3,512,128]{1,2,0:T(8,128)(2,1)} %copy-done) | copy-start | bytes 1179652
  78.4 176.4 %reduce-scatter.5.cloned.1.call-start = ((), (), s32[]{:S(2)}) async-start(), calls=%async_computation.8 | async-start | bytes 9437184 | tf_op jit(solution)/shard_map/reduce_scatter | solution.py:139
  89.4 10.7 %all-to-all-start.3 = ((bf16[64,8,128]{2,0,1:T(8,128)(2,1)}), bf16[64,8,128]{2,0,1:T(8,128)(2,1)S(1)}, u32[]{:S(2)}, u32[]{:S(2)}) async-start(bf16[64,8,128]{2,0,1:T(8,128)(2,1)} %copy.66), calls=%async_computation.4 | async-start | bytes 262144 | tf_op jit(solution)/shard_map/all_to_all | solution.py:108
  101.3 5.7 %collective-permute-start.1 = (bf16[3,512,6]{1,2,0:T(8,128)(2,1)S(1)}, bf16[3,512,6]{1,2,0:T(8,128)(2,1)S(1)}, u32[]{:S(2)}, u32[]{:S(2)}) collective-permute-start(bf16[3,512,6]{1,2,0:T(8,128)(2,1)S(1)} %pad_maximum_fusion), channel_id=1, source_target_pairs={{4,0},{8,4},{12,8},{16,12},{20,16},{24,20},{28,24},{5,1},{9,5},{13... | collective-permute-start | bytes 55304 | tf_op jit(solution)/shard_map/ppermute | solution.py:18
Sparse Core Ops, SparseCore 0:
  9.6 19.4 all-gather.1
  78.6 22.7 reduce-scatter.2
  105.4 149.3 reduce-scatter.4
where the time goes:
time: 265 us; the launch traced here: 264 us
  waiting for transfers between devices  161 us (61%)
  matrix products  43.3 us (16%)
  starting transfers between devices  18.3 us (7%)
  between operations  14.3 us (5%)
  local copies, waits for them, and re-layouts  14 us (5%)
  blocking collectives  9.74 us (4%)
  other arithmetic  2.84 us (1%)
    reduce_scatter x1, waiting for transfers between devices, per_device(): lax.psum_scatter(lax.dot_general(full_cotangent, gated_out, (((1,), (1,))...  143 us
    all_to_all x2, waiting for transfers between devices, to_channels(): return lax.all_to_all(block, 'ctx', split_axis=0, concat_axis=1, tiled=True)  11.1 us
    unnamed x27, local copies, waits for them, and re-layouts  10.7 us
    all_to_all x1, blocking collectives, to_positions(): return lax.all_to_all(block, 'ctx', split_axis=1, concat_axis=0, tiled=True)  9.74 us
    all_to_all x2, starting transfers between devices, to_channels(): return lax.all_to_all(block, 'ctx', split_axis=0, concat_axis=1, tiled=True)  8.25 us
    ppermute x2, starting transfers between devices, from_behind(): lax.ppermute(value, axis, [(source, source + steps) for source in range(f...  6.14 us
    dot_general x1, matrix products, per_device(): lax.dot_general(full_cotangent, gated_out, (((1,), (1,)), ((), ())), pref...  5.79 us
  transfers between devices with their start and end apart: 8, of which 5 were waited for; matrix products, arithmetic and copies ran while one was open for 15% of the time, Pallas kernels for 0%

commit v1 on v0

v1 whole, which is shorter than its diff:
```python
import functools

import jax
import jax.numpy as jnp
import numpy as np
from jax import lax
from jax.experimental import pallas as pl
from jax.experimental.pallas import tpu as pltpu
from jax.sharding import PartitionSpec as P

F32 = jnp.float32
BF16 = jnp.bfloat16
MESH = pl.DeviceIdType.MESH


def split_table(table):
    table = table.astype(np.float32)
    high = table.astype(jnp.bfloat16)
    low = (table - high.astype(np.float32)).astype(jnp.bfloat16)
    return high, low


def make_tables(blocks, width):
    rows = 2 * blocks
    full = rows * width
    kept = blocks + 1
    turn = np.outer(np.arange(kept), np.arange(blocks)) % rows * (2 * np.pi / rows)
    outer = np.stack([np.cos(turn), -np.sin(turn)]).astype(np.float32)
    twist = np.outer(np.arange(kept), np.arange(width)) % full * (2 * np.pi / full)
    weight = np.full((kept, 1), 2.0 / full)
    weight[0] = weight[-1] = 1.0 / full
    twists = np.stack(
        [np.cos(twist), -np.sin(twist), weight * np.cos(twist), weight * -np.sin(twist)]
    ).astype(np.float32)[:, :, None, :]
    inner = np.outer(np.arange(width), np.arange(width)) % width * (2 * np.pi / width)
    re, im = np.cos(inner), -np.sin(inner)
    forward = np.block([[re, im], [-im, re]])
    backward = np.block([[re, -im], [im, re]])
    return outer, twists, *split_table(forward), *split_table(backward)


def dot(a, b):
    return jnp.dot(a, b, preferred_element_type=F32)


def dot_split(value, high, low):
    value_high = value.astype(BF16)
    value_low = (value - value_high.astype(F32)).astype(BF16)
    return dot(value_high, high) + dot(value_low, high) + dot(value_high, low)


def merge_rows(value):
    blocks, rows, lanes = value.shape
    if rows % 16:
        return value.astype(F32).reshape(blocks * rows, lanes).astype(BF16)
    return value.reshape(blocks * rows, lanes)


def kernel(
    nctx,
    ntp,
    outer,
    query,
    key,
    value,
    taps,
    filters,
    weight_hbm,
    cot,
    twists,
    fwd_high,
    fwd_low,
    bwd_high,
    bwd_low,
    mixed_out,
    grad_query,
    grad_key,
    grad_value,
    grad_filters,
    grad_weight,
    weight,
    full_cot,
    cot_rows,
    inputs,
    shorts,
    signal,
    work,
    parts,
    spec_f,
    spec_p,
    spec_g,
    convolved,
    gated,
    gated_here,
    gated_all,
    gate_out,
    gate_chan,
    shorts_grad,
    grads,
    partial,
    pair_in,
    pair_sum,
    final_in,
    local_sem,
    in_s,
    in_r,
    cot_s,
    cot_r,
    rows_s,
    rows_r,
    quart_s,
    quart_r,
    gate_s,
    gate_r,
    here_s,
    here_r,
    all_s,
    all_r,
    fwd_s,
    fwd_r,
    back_s,
    back_r,
    pair_s,
    pair_r,
    final_s,
    final_r,
):
    channels, width = query.shape[1:]
    kept = nctx + 1
    tap_count = taps.shape[3]
    me = lax.axis_index("ctx")
    mine = lax.axis_index("tp")
    core_mate = mine + 1 - 2 * (mine % 2)
    side_mate = (mine + ntp // 2) % ntp
    far_mate = (core_mate + ntp // 2) % ntp
    x_mate = me + 1 - 2 * (me % 2)
    share = nctx // ntp

    def send(src, dst, send_sem, recv_sem, device):
        copy = pltpu.make_async_remote_copy(
            src_ref=src,
            dst_ref=dst,
            send_sem=send_sem,
            recv_sem=recv_sem,
            device_id=device,
            device_id_type=MESH,
        )
        copy.start()
        return copy

    def peer(step):
        return lax.rem(me + step, nctx)

    def at_ctx(target):
        return (target, mine)

    def at_tp(target):
        return (me, target)

    load_weight = pltpu.make_async_copy(weight_hbm, weight, local_sem)
    load_weight.start()

    barrier = pltpu.get_barrier_semaphore()
    for step in range(1, nctx):
        pl.semaphore_signal(barrier, inc=1, device_id=at_ctx(peer(step)), device_id_type=MESH)
    for mate in (core_mate, side_mate):
        pl.semaphore_signal(barrier, inc=1, device_id=at_tp(mate), device_id_type=MESH)
    pl.semaphore_wait(barrier, nctx + 1)

    sent = []

    own_rows = full_cot.at[pl.ds(mine * share, share)]
    to_side = send(cot, own_rows, cot_s.at[0], cot_r.at[0], at_tp(side_mate))
    to_core = send(cot, own_rows, cot_s.at[1], cot_r.at[1], at_tp(core_mate))
    sent += [to_side, to_core]
    in_copies = []
    for step in range(1, nctx):
        target = peer(step)
        for index, source in enumerate((query, key, value)):
            copy = send(
                source.at[target],
                inputs.at[index, me + 1],
                in_s.at[index, step],
                in_r.at[index, step],
                at_ctx(target),
            )
            in_copies.append(copy)
    sent += in_copies
    for index, source in enumerate((query, key, value)):
        inputs[index, me + 1] = source[me]
        inputs[index, 0] = jnp.zeros((channels, width), BF16)
        shorts_grad[index, nctx] = jnp.zeros((channels, width), BF16)
    full_cot[pl.ds(mine * share, share)] = cot[...]

    def spectrum(spec):
        def one(k, carry):
            re = jnp.zeros((channels, width), F32)
            im = jnp.zeros((channels, width), F32)
            for n in range(nctx):
                block = signal[n]
                re = re + outer[0, k, n] * block
                im = im + outer[1, k, n] * block
            cos, sin = twists[0, k], twists[1, k]
            rows = pl.ds(pl.multiple_of(k * channels, channels), channels)
            work[rows, :width] = re * cos - im * sin
            work[rows, width:] = re * sin + im * cos
            return carry

        lax.fori_loop(0, kept, one, 0)
        spec[...] = dot_split(work[...], fwd_high[...], fwd_low[...])

    def inverse(re, im, store):
        work[:, :width] = re
        work[:, width:] = im
        work[...] = dot_split(work[...], bwd_high[...], bwd_low[...])

        def turn(k, carry):
            rows = pl.ds(pl.multiple_of(k * channels, channels), channels)
            back_re, back_im = work[rows, :width], work[rows, width:]
            cos, sin = twists[2, k], twists[3, k]
            parts[0, k] = back_re * cos + back_im * sin
            parts[1, k] = back_im * cos - back_re * sin
            return carry

        lax.fori_loop(0, kept, turn, 0)

        def one(n, carry):
            total = parts[0, 0]
            for k in range(1, kept):
                total = total + outer[0, k, n] * parts[0, k]
                if k < nctx:
                    total = total + outer[1, k, n] * parts[1, k]
            store(n, total)
            return carry

        lax.fori_loop(0, nctx, one, 0)

    lane = lax.broadcasted_iota(jnp.int32, (channels, width), 1)

    for n in range(nctx):
        signal[n] = filters[:, n * width : (n + 1) * width]
    spectrum(spec_f)

    to_side.wait_recv()
    passed_rows = full_cot.at[pl.ds(side_mate * share, share)]
    passed = send(passed_rows, passed_rows, cot_s.at[2], cot_r.at[2], at_tp(core_mate))
    sent.append(passed)
    to_core.wait_recv()
    load_weight.wait()
    passed.wait_recv()

    block_rows = cot.shape[0] * cot.shape[1] * cot.shape[2]
    total = jnp.zeros((width, nctx * channels), F32)
    for group in range(ntp):
        cot_block = full_cot[group * share : (group + 1) * share].reshape(block_rows, width)
        total = total + lax.dot_general(
            cot_block,
            weight[group * block_rows : (group + 1) * block_rows, :],
            (((0,), (0,)), ((), ())),
            preferred_element_type=F32,
        )
    gate_out[...] = total.T.reshape(nctx, channels, width).astype(BF16)
    gate_copies = []
    for step in range(1, nctx):
        target = peer(step)
        gate_copies.append(
            send(
                gate_out.at[target],
                gate_chan.at[me],
                gate_s.at[step],
                gate_r.at[step],
                at_ctx(target),
            )
        )
    sent += gate_copies
    gate_chan[me] = gate_out[me]

    for copy in in_copies:
        copy.wait_recv()

    row_copies = []
    for step in range(1, nctx):
        target = peer(step)
        row_copies.append(
            send(
                full_cot.at[target, mine],
                cot_rows.at[mine, me],
                rows_s.at[step],
                rows_r.at[step],
                at_ctx(target),
            )
        )
    sent += row_copies
    cot_rows[mine, me] = full_cot[me, mine]

    for index in range(3):
        tap = taps[index, me]

        def short(n, carry, index=index, tap=tap):
            before = inputs[index, n].astype(F32)
            here = inputs[index, n + 1].astype(F32)
            total = tap[:, 0:1] * here
            for j in range(1, tap_count):
                moved = jnp.where(lane < j, pltpu.roll(before, j, 1), pltpu.roll(here, j, 1))
                total = total + tap[:, j : j + 1] * moved
            shorts[index, n] = total.astype(BF16)
            return carry

        lax.fori_loop(0, nctx, short, 0)

    def multiply(n, carry):
        product = shorts[1, n].astype(F32) * shorts[2, n].astype(F32)
        signal[n] = product.astype(BF16).astype(F32)
        return carry

    lax.fori_loop(0, nctx, multiply, 0)
    spectrum(spec_p)

    f_re, f_im = spec_f[:, :width], spec_f[:, width:]
    p_re, p_im = spec_p[:, :width], spec_p[:, width:]

    def store_convolved(n, total):
        rounded = total.astype(BF16)
        convolved[n] = rounded
        gated[n] = (shorts[0, n].astype(F32) * rounded.astype(F32)).astype(BF16)

    inverse(p_re * f_re - p_im * f_im, p_re * f_im + p_im * f_re, store_convolved)

    here_copies = []
    for step in range(1, nctx):
        target = peer(step)
        here_copies.append(
            send(
                gated.at[target],
                gated_here.at[me],
                here_s.at[step],
                here_r.at[step],
                at_ctx(target),
            )
        )
    sent += here_copies
    to_x = send(gated, gated_all.at[me], fwd_s.at[0], fwd_r.at[0], at_ctx(x_mate))
    all_copies = [
        send(gated, gated_all.at[me], all_s.at[step], all_r.at[step], at_ctx(peer(step)))
        for step in range(2, nctx, 2)
    ]
    sent += [to_x] + all_copies
    gated_here[me] = gated[me]
    gated_all[me] = gated[...]

    for copy in row_copies:
        copy.wait_recv()
    own_quarter = cot_rows.at[mine]
    quarter_side = send(own_quarter, own_quarter, quart_s.at[0], quart_r.at[0], at_tp(side_mate))
    quarter_core = send(own_quarter, own_quarter, quart_s.at[1], quart_r.at[1], at_tp(core_mate))
    sent += [quarter_side, quarter_core]

    for copy in gate_copies:
        copy.wait_recv()

    def to_conv(n, carry):
        grad_conv = gate_chan[n].astype(F32) * shorts[0, n].astype(F32)
        signal[n] = grad_conv.astype(BF16).astype(F32)
        return carry

    lax.fori_loop(0, nctx, to_conv, 0)
    spectrum(spec_g)

    for copy in here_copies:
        copy.wait_recv()
    right = merge_rows(gated_here[...])

    def project(group):
        start = pl.multiple_of(group * block_rows, block_rows)
        return dot(weight[pl.ds(start, block_rows), :], right)

    core = mine % 2
    pair_copies = []
    for side in range(ntp // 2):
        partial[side] = project(2 * side + 1 - core).astype(BF16)
        pair_copies.append(
            send(
                partial.at[side],
                pair_in.at[side],
                pair_s.at[side],
                pair_r.at[side],
                at_tp(core_mate),
            )
        )
    sent += pair_copies

    f_re, f_im = spec_f[:, :width], spec_f[:, width:]
    g_re, g_im = spec_g[:, :width], spec_g[:, width:]

    def store_product(n, total):
        rounded = total.astype(BF16).astype(F32)
        gate = gate_chan[n].astype(F32)
        shorts_grad[0, n] = (gate * convolved[n].astype(F32)).astype(BF16)
        shorts_grad[1, n] = (rounded * shorts[2, n].astype(F32)).astype(BF16)
        shorts_grad[2, n] = (rounded * shorts[1, n].astype(F32)).astype(BF16)

    inverse(f_re * g_re + f_im * g_im, f_re * g_im - f_im * g_re, store_product)

    for index in range(3):
        tap = taps[index, me]

        def long(n, carry, index=index, tap=tap):
            here = shorts_grad[index, n].astype(F32)
            after = shorts_grad[index, n + 1].astype(F32)
            total = tap[:, 0:1] * here
            for j in range(1, tap_count):
                moved = jnp.where(
                    lane < width - j,
                    pltpu.roll(here, width - j, 1),
                    pltpu.roll(after, width - j, 1),
                )
                total = total + tap[:, j : j + 1] * moved
            grads[index, n] = total.astype(BF16)
            return carry

        lax.fori_loop(0, nctx, long, 0)
    results = (grad_query, grad_key, grad_value)
    back_copies = []
    for step in range(1, nctx):
        target = peer(step)
        for index, result in enumerate(results):
            back_copies.append(
                send(
                    grads.at[index, target],
                    result.at[me],
                    back_s.at[index, step],
                    back_r.at[index, step],
                    at_ctx(target),
                )
            )
    sent += back_copies
    for index, result in enumerate(results):
        result[me] = grads[index, me]

    my_side = mine // 2
    for copy in pair_copies:
        copy.wait_recv()
    other = 1 - my_side
    pair_sum[...] = (project(side_mate) + pair_in[other].astype(F32)).astype(BF16)
    final = send(pair_sum, final_in, final_s, final_r, at_tp(side_mate))
    sent.append(final)

    passed_all = []
    for copy, step in zip(all_copies, range(2, nctx, 2)):
        copy.wait_recv()
        block = gated_all.at[lax.rem(me + nctx - step, nctx)]
        passed_all.append(
            send(block, block, fwd_s.at[step // 2], fwd_r.at[step // 2], at_ctx(x_mate))
        )
    sent += passed_all
    quarter_side.wait_recv()
    far_quarter = cot_rows.at[side_mate]
    quarter_far = send(far_quarter, far_quarter, quart_s.at[2], quart_r.at[2], at_tp(core_mate))
    sent.append(quarter_far)

    own_sum = project(mine) + pair_in[my_side].astype(F32)

    p_re, p_im = spec_p[:, :width], spec_p[:, width:]
    g_re, g_im = spec_g[:, :width], spec_g[:, width:]

    def store_filters(n, total):
        grad_filters[:, pl.ds(pl.multiple_of(n * width, width), width)] = total

    inverse(p_re * g_re + p_im * g_im, p_re * g_im - p_im * g_re, store_filters)

    final.wait_recv()
    mixed_out[...] = (own_sum + final_in[...].astype(F32)).astype(BF16)

    quarter_core.wait_recv()
    quarter_far.wait_recv()
    to_x.wait_recv()
    for copy in passed_all:
        copy.wait_recv()
    quarter = cot_rows.shape[2]

    def weigh(n, totals):
        right = merge_rows(gated_all[:, n])
        left = cot_rows[:, n].reshape(ntp * quarter, width)
        grad_weight[...] += lax.dot_general(
            left, right, (((1,), (1,)), ((), ())), preferred_element_type=F32
        )
        return totals

    grad_weight[...] = jnp.zeros_like(grad_weight)
    lax.fori_loop(0, nctx, weigh, 0)

    for copy in back_copies:
        copy.wait_recv()
    for copy in sent:
        copy.wait_send()


def per_device(nctx, ntp, query_in, key_in, value_in, short_weights, filters, out_weight, cotangent):
    rows, width = query_in.shape
    channels = rows // nctx
    features = out_weight.shape[0]
    quarter = features // (nctx * ntp)
    share = nctx // ntp
    kept = nctx + 1
    outer, twists, *inner = make_tables(nctx, width)
    tap_count = short_weights.shape[2]
    blocks = (nctx, channels, width)

    def bf(*shape):
        return pltpu.VMEM(shape, BF16)

    def f32(*shape):
        return pltpu.VMEM(shape, F32)

    def sems(*shape):
        return pltpu.SemaphoreType.DMA(shape)

    vmem = pl.BlockSpec(memory_space=pltpu.VMEM)
    smem = pl.BlockSpec(memory_space=pltpu.SMEM)
    outs = pl.pallas_call(
        functools.partial(kernel, nctx, ntp),
        out_shape=(
            jax.ShapeDtypeStruct((features // ntp, width), BF16),
            jax.ShapeDtypeStruct(blocks, BF16),
            jax.ShapeDtypeStruct(blocks, BF16),
            jax.ShapeDtypeStruct(blocks, BF16),
            jax.ShapeDtypeStruct((channels, nctx * width), F32),
            jax.ShapeDtypeStruct((features // nctx, rows), F32),
        ),
        in_specs=[smem] + [vmem] * 5 + [pl.BlockSpec(memory_space=pl.ANY)] + [vmem] * 6,
        out_specs=tuple([vmem] * 6),
        scratch_shapes=[
            bf(features, rows),
            bf(nctx, ntp, quarter, width),
            bf(ntp, nctx, quarter, width),
            bf(3, nctx + 1, channels, width),
            bf(3, *blocks),
            f32(*blocks),
            f32(kept * channels, 2 * width),
            f32(2, kept, channels, width),
            f32(kept * channels, 2 * width),
            f32(kept * channels, 2 * width),
            f32(kept * channels, 2 * width),
            bf(*blocks),
            bf(*blocks),
            bf(*blocks),
            bf(nctx, *blocks),
            bf(*blocks),
            bf(*blocks),
            bf(3, nctx + 1, channels, width),
            bf(3, *blocks),
            bf(ntp // 2, features // ntp, width),
            bf(ntp // 2, features // ntp, width),
            bf(features // ntp, width),
            bf(features // ntp, width),
            pltpu.SemaphoreType.DMA,
            sems(3, nctx),
            sems(3, nctx),
            sems(3),
            sems(3),
            sems(nctx),
            sems(nctx),
            sems(3),
            sems(3),
            sems(nctx),
            sems(nctx),
            sems(nctx),
            sems(nctx),
            sems(nctx),
            sems(nctx),
            sems(nctx),
            sems(nctx),
            sems(3, nctx),
            sems(3, nctx),
            sems(ntp // 2),
            sems(ntp // 2),
            pltpu.SemaphoreType.DMA,
            pltpu.SemaphoreType.DMA,
        ],
        compiler_params=pltpu.CompilerParams(
            collective_id=0, has_side_effects=True, vmem_limit_bytes=56 * 1024 * 1024
        ),
        cost_estimate=pl.CostEstimate(
            flops=6 * features * rows * width, bytes_accessed=10 * features * rows // 4, transcendentals=0
        ),
        name="mixer",
    )(
        jnp.asarray(outer),
        query_in.reshape(blocks),
        key_in.reshape(blocks),
        value_in.reshape(blocks),
        short_weights.reshape(3, nctx, channels, tap_count),
        filters.reshape(channels, nctx * width),
        out_weight,
        cotangent.reshape(share, ntp, quarter, width),
        jnp.asarray(twists),
        *[jnp.asarray(table) for table in inner],
    )
    mixed, grad_query, grad_key, grad_value, grad_filters, grad_weight = outs
    return (
        mixed,
        grad_query.reshape(rows, width),
        grad_key.reshape(rows, width),
        grad_value.reshape(rows, width),
        grad_filters.reshape(filters.shape),
        grad_weight,
    )


def solution(mesh):
    placed = (
        P("tp", "ctx"),
        P("tp", "ctx"),
        P("tp", "ctx"),
        P(None, "tp", None),
        P("tp", "ctx", None),
        P(None, "tp"),
        P("tp", "ctx"),
    )
    return jax.shard_map(
        functools.partial(per_device, mesh.shape["ctx"], mesh.shape["tp"]),
        mesh=mesh,
        in_specs=placed,
        out_specs=(
            P("tp", "ctx"),
            P("tp", "ctx"),
            P("tp", "ctx"),
            P("tp", "ctx"),
            P("tp", "ctx", None),
            P("ctx", "tp"),
        ),
        check_vma=False,
    )
```

time: 265 us -> 74.7 us (0.28)
  waiting for transfers between devices: 161 us -> 0 us
  Pallas kernels: 0 us -> 61.4 us
  matrix products: 43.3 us -> 0 us
  starting transfers between devices: 18.3 us -> 0 us
  between operations: 14.3 us -> 0.64 us
  blocking collectives: 9.74 us -> 0 us
  other arithmetic: 2.84 us -> 0 us
    reduce_scatter x2 -> x0, waiting for transfers between devices: 143 us -> none  [the longest x1 143 us: per_device(): lax.psum_scatter(lax.dot_general(full_cotangent, gated_out, (((1,), (1,))...]
    pallas_call x0 -> x1, Pallas kernels: none -> 61.4 us  [per_device(): pl.pallas_call(functools.partial(kernel, nctx, ntp), out_shape=(jax.Shape...]
    dot_general x39 -> x0, matrix products: 43.3 us -> none  [the longest x1 5.79 us: per_device(): lax.dot_general(full_cotangent, gated_out, (((1,), (1,)), ((), ())), pref...]
    all_to_all x3 -> x0, waiting for transfers between devices: 14.6 us -> none  [the longest x2 11.1 us: to_channels(): return lax.all_to_all(block, 'ctx', split_axis=0, concat_axis=1, tiled=True)]
    all_to_all x3 -> x0, starting transfers between devices: 11.6 us -> none  [the longest x2 8.25 us: to_channels(): return lax.all_to_all(block, 'ctx', split_axis=0, concat_axis=1, tiled=True)]
    all_to_all x1 -> x0, blocking collectives: 9.74 us -> none  [to_positions(): return lax.all_to_all(block, 'ctx', split_axis=1, concat_axis=0, tiled=True)]
    ppermute x2 -> x0, starting transfers between devices: 6.14 us -> none  [from_behind(): lax.ppermute(value, axis, [(source, source + steps) for source in range(f...]
    ppermute x2 -> x0, waiting for transfers between devices: 3.2 us -> none  [from_behind(): lax.ppermute(value, axis, [(source, source + steps) for source in range(f...]
  transfers between devices with their start and end apart: 8 -> 0, of which waited for: 5 -> 0; matrix products, arithmetic and copies ran while one was open for 15% -> 0% of each run, Pallas kernels for 0% -> 0%
where the time goes in v1:
time: 74.7 us; the launch traced here: 74.3 us
  Pallas kernels  61.4 us (82%)
  local copies, waits for them, and re-layouts  12.3 us (16%)
    pallas_call x1, Pallas kernels, per_device(): pl.pallas_call(functools.partial(kernel, nctx, ntp), out_shape=(jax.Shape...  61.4 us
    unnamed x7, local copies, waits for them, and re-layouts  12.3 us

profile of v1, /device:TPU:0, one launch (start us, length us, event | category | flops | bytes accessed | tf_op | source)
XLA Modules:
  0.0 74.3 jit_solution(13779667503127158538)
XLA Ops:
  0.6 2.0 %copy.19 = f32[3,512,7]{2,1,0:T(8,128)} copy(f32[3,512,7]{1,2,0:T(8,128)} %param.16) | data formatting | bytes 86016 | tf_op args[3]
  2.6 61.4 %mixer.1 = (bf16[1024,128]{1,0:T(8,128)(2,1)}, bf16[8,64,128]{2,1,0:T(8,128)(2,1)}, bf16[8,64,128]{2,1,0:T(8,128)(2,1)}, bf16[8,64,128]{2,1,0:T(8,128)(2,1)}, f32[64,1024]{1,0:T(8,128)}, /*index=5*/f32[512,512]{1,0:T(8,128)}) custom-call(f32[2,9,8]{2,1,0:T(8,128)} %constant.12.clone.outer, bf16[8,64,128]{2,1,0:T(8,128)(2,1)} %bitcast.14, ...), custom_call_target="tpu_custom_call" | custom-call | flops 1610612736 | bytes 5242880 | tf_op jit(solution)/shard_map/mixer/pallas_call | solution.py:520
  64.0 1.7 %copy.26 = bf16[1024,128]{1,0:T(8,128)(2,1)} copy(bf16[1024,128]{1,0:T(8,128)(2,1)} %get-tuple-element.24) | data formatting | bytes 524288
  65.7 1.6 %copy.27 = bf16[512,128]{1,0:T(8,128)(2,1)} copy(bf16[512,128]{1,0:T(8,128)(2,1)} %bitcast.19) | data formatting | bytes 262144
  67.2 1.6 %copy.28 = bf16[512,128]{1,0:T(8,128)(2,1)} copy(bf16[512,128]{1,0:T(8,128)(2,1)} %bitcast.18) | data formatting | bytes 262144
  68.8 1.6 %copy.29 = bf16[512,128]{1,0:T(8,128)(2,1)} copy(bf16[512,128]{1,0:T(8,128)(2,1)} %bitcast.17) | data formatting | bytes 262144
  70.4 1.7 %copy.30 = f32[1,64,1024]{2,1,0:T(8,128)} copy(f32[1,64,1024]{2,1,0:T(8,128)} %bitcast.13) | data formatting | bytes 524288
  72.0 2.3 %copy.31 = f32[512,512]{1,0:T(8,128)} copy(f32[512,512]{1,0:T(8,128)} %get-tuple-element.29) | data formatting | bytes 2097152

commit v2 on v1

v2 whole, which is shorter than its diff:
```python
import functools

import jax
import jax.numpy as jnp
import numpy as np
from jax import lax
from jax.experimental import pallas as pl
from jax.experimental.pallas import tpu as pltpu
from jax.sharding import PartitionSpec as P

F32 = jnp.float32
BF16 = jnp.bfloat16
MESH = pl.DeviceIdType.MESH


def split_table(table):
    table = table.astype(np.float32)
    high = table.astype(jnp.bfloat16)
    low = (table - high.astype(np.float32)).astype(jnp.bfloat16)
    return high, low


def make_tables(blocks, width):
    rows = 2 * blocks
    full = rows * width
    kept = blocks + 1
    turn = np.outer(np.arange(kept), np.arange(blocks)) % rows * (2 * np.pi / rows)
    outer = np.stack([np.cos(turn), -np.sin(turn)]).astype(np.float32)
    twist = np.outer(np.arange(kept), np.arange(width)) % full * (2 * np.pi / full)
    weight = np.full((kept, 1), 2.0 / full)
    weight[0] = weight[-1] = 1.0 / full
    twists = np.stack(
        [np.cos(twist), -np.sin(twist), weight * np.cos(twist), weight * -np.sin(twist)]
    ).astype(np.float32)[:, :, None, :]
    inner = np.outer(np.arange(width), np.arange(width)) % width * (2 * np.pi / width)
    re, im = np.cos(inner), -np.sin(inner)
    forward = np.block([[re, im], [-im, re]])
    backward = np.block([[re, -im], [im, re]])
    return outer, twists, *split_table(forward), *split_table(backward)


def dot(a, b):
    return jnp.dot(a, b, preferred_element_type=F32)


def dot_split(value, high, low):
    value_high = value.astype(BF16)
    value_low = (value - value_high.astype(F32)).astype(BF16)
    return dot(value_high, high) + dot(value_low, high) + dot(value_high, low)


def merge_rows(value):
    blocks, rows, lanes = value.shape
    if rows % 16:
        return value.astype(F32).reshape(blocks * rows, lanes).astype(BF16)
    return value.reshape(blocks * rows, lanes)


def kernel(
    nctx,
    ntp,
    outer,
    query,
    key,
    value,
    taps_in,
    filters,
    weight_hbm,
    cot,
    ends,
    starts,
    twists,
    fwd_high,
    fwd_low,
    bwd_high,
    bwd_low,
    mixed_out,
    grad_query,
    grad_key,
    grad_value,
    grad_filters,
    grad_weight,
    weight,
    full_cot,
    cot_rows,
    taps,
    halo_out,
    halo_in,
    edge,
    shorts,
    signal,
    work,
    parts,
    spec_f,
    spec_p,
    spec_g,
    product,
    product_chan,
    conv_chan,
    conv_here,
    gated_all,
    grad_gated,
    grad_conv,
    grad_conv_chan,
    grad_chan,
    grad_here,
    shorts_grad,
    partial,
    pair_in,
    pair_sum,
    final_in,
    local_sem,
    halo_s,
    halo_r,
    cot_s,
    cot_r,
    rows_s,
    rows_r,
    quart_s,
    quart_r,
    product_s,
    product_r,
    conv_s,
    conv_r,
    grad_s,
    grad_r,
    back_s,
    back_r,
    all_s,
    all_r,
    fwd_s,
    fwd_r,
    pair_s,
    pair_r,
    final_s,
    final_r,
):
    channels, width = query.shape[1:]
    kept = nctx + 1
    tap_count = taps_in.shape[1]
    me = lax.axis_index("ctx")
    mine = lax.axis_index("tp")
    core_mate = mine + 1 - 2 * (mine % 2)
    side_mate = (mine + ntp // 2) % ntp
    far_mate = (core_mate + ntp // 2) % ntp
    x_mate = me + 1 - 2 * (me % 2)
    share = nctx // ntp
    block_rows = cot.shape[0] * cot.shape[1] * cot.shape[2]

    def send(src, dst, send_sem, recv_sem, device):
        copy = pltpu.make_async_remote_copy(
            src_ref=src,
            dst_ref=dst,
            send_sem=send_sem,
            recv_sem=recv_sem,
            device_id=device,
            device_id_type=MESH,
        )
        copy.start()
        return copy

    def peer(step):
        return lax.rem(me + step, nctx)

    def at_ctx(target):
        return (target, mine)

    def at_tp(target):
        return (me, target)

    def exchange(source, dest, send_sem, recv_sem):
        copies = []
        for step in range(1, nctx):
            target = peer(step)
            copies.append(
                send(
                    source.at[target],
                    dest.at[me],
                    send_sem.at[step],
                    recv_sem.at[step],
                    at_ctx(target),
                )
            )
        dest[me] = source[me]
        return copies

    def wait_all(copies):
        for copy in copies:
            copy.wait_recv()

    load_weight = pltpu.make_async_copy(weight_hbm, weight, local_sem)
    load_weight.start()

    barrier = pltpu.get_barrier_semaphore()
    for step in range(1, nctx):
        pl.semaphore_signal(barrier, inc=1, device_id=at_ctx(peer(step)), device_id_type=MESH)
    for mate in (core_mate, side_mate):
        pl.semaphore_signal(barrier, inc=1, device_id=at_tp(mate), device_id_type=MESH)

    def pack_edges(picks, sources):
        total = None
        for index, source in enumerate(sources):
            block = merge_rows(source[...])
            term = lax.dot_general(
                picks[index], block, (((1,), (1,)), ((), ())), preferred_element_type=F32
            )
            total = term if total is None else total + term
        halo_out[...] = total.astype(BF16)

    def unpack_edges(picks):
        for index in range(3):
            spread = lax.dot_general(
                halo_in[...], picks[index], (((0,), (0,)), ((), ())), preferred_element_type=F32
            )
            edge[index] = spread.reshape(nctx, channels, width)

    pack_edges(ends, (query, key, value))
    pl.semaphore_wait(barrier, nctx + 1)

    sent = []
    halo = send(halo_out, halo_in, halo_s.at[0], halo_r.at[0], at_ctx(peer(1)))
    own_rows = full_cot.at[pl.ds(mine * share, share)]
    to_side = send(cot, own_rows, cot_s.at[0], cot_r.at[0], at_tp(side_mate))
    to_core = send(cot, own_rows, cot_s.at[1], cot_r.at[1], at_tp(core_mate))
    sent += [to_side, to_core]
    full_cot[pl.ds(mine * share, share)] = cot[...]
    for index in range(3):
        padded = jnp.concatenate(
            [taps_in[index], jnp.zeros((taps.shape[3] - tap_count, nctx * channels), F32)], axis=0
        )
        taps[index] = padded.T.reshape(nctx, channels, taps.shape[3])

    def spectrum(spec):
        def one(k, carry):
            re = jnp.zeros((channels, width), F32)
            im = jnp.zeros((channels, width), F32)
            for n in range(nctx):
                block = signal[n]
                re = re + outer[0, k, n] * block
                im = im + outer[1, k, n] * block
            cos, sin = twists[0, k], twists[1, k]
            rows = pl.ds(pl.multiple_of(k * channels, channels), channels)
            work[rows, :width] = re * cos - im * sin
            work[rows, width:] = re * sin + im * cos
            return carry

        lax.fori_loop(0, kept, one, 0)
        spec[...] = dot_split(work[...], fwd_high[...], fwd_low[...])

    def inverse(re, im, store):
        work[:, :width] = re
        work[:, width:] = im
        work[...] = dot_split(work[...], bwd_high[...], bwd_low[...])

        def turn(k, carry):
            rows = pl.ds(pl.multiple_of(k * channels, channels), channels)
            back_re, back_im = work[rows, :width], work[rows, width:]
            cos, sin = twists[2, k], twists[3, k]
            parts[0, k] = back_re * cos + back_im * sin
            parts[1, k] = back_im * cos - back_re * sin
            return carry

        lax.fori_loop(0, kept, turn, 0)

        def one(n, carry):
            total = parts[0, 0]
            for k in range(1, kept):
                total = total + outer[0, k, n] * parts[0, k]
                if k < nctx:
                    total = total + outer[1, k, n] * parts[1, k]
            store(n, total)
            return carry

        lax.fori_loop(0, nctx, one, 0)

    lane = lax.broadcasted_iota(jnp.int32, (channels, width), 1)

    for n in range(nctx):
        signal[n] = filters[:, n * width : (n + 1) * width]
    spectrum(spec_f)

    halo.wait()
    unpack_edges(ends)
    has_before = me > 0

    def short(index):
        source = (query, key, value)[index]

        def one(m, carry):
            tap = taps[index, m]
            here = source[m].astype(F32)
            before = jnp.where(has_before, edge[index, m], 0.0)
            total = tap[:, 0:1] * here
            for j in range(1, tap_count):
                moved = pltpu.roll(jnp.where(lane >= width - j, before, here), j, 1)
                total = total + tap[:, j : j + 1] * moved
            shorts[index, m] = total.astype(BF16)
            return carry

        lax.fori_loop(0, nctx, one, 0)

    short(1)
    short(2)
    product[...] = (shorts[1].astype(F32) * shorts[2].astype(F32)).astype(BF16)
    product_copies = exchange(product, product_chan, product_s, product_r)
    sent += product_copies
    short(0)

    to_side.wait_recv()
    passed_rows = full_cot.at[pl.ds(side_mate * share, share)]
    passed = send(passed_rows, passed_rows, cot_s.at[2], cot_r.at[2], at_tp(core_mate))
    sent.append(passed)
    load_weight.wait()
    to_core.wait_recv()

    def gate_part(group):
        cot_block = full_cot[pl.ds(group * share, share)].reshape(block_rows, width)
        start = pl.multiple_of(group * block_rows, block_rows)
        return lax.dot_general(
            cot_block,
            weight[pl.ds(start, block_rows), :],
            (((0,), (0,)), ((), ())),
            preferred_element_type=F32,
        )

    total = gate_part(mine) + gate_part(core_mate) + gate_part(side_mate)
    passed.wait_recv()
    total = total + gate_part(far_mate)
    grad_gated[...] = total.T.reshape(nctx, channels, width)
    grad_conv[...] = (grad_gated[...] * shorts[0].astype(F32)).astype(BF16)
    grad_copies = exchange(grad_conv, grad_conv_chan, grad_s, grad_r)
    sent += grad_copies

    wait_all(product_copies)
    signal[...] = product_chan[...].astype(F32)
    spectrum(spec_p)

    f_re, f_im = spec_f[:, :width], spec_f[:, width:]
    p_re, p_im = spec_p[:, :width], spec_p[:, width:]

    def store_convolved(n, total):
        conv_chan[n] = total.astype(BF16)

    inverse(p_re * f_re - p_im * f_im, p_re * f_im + p_im * f_re, store_convolved)
    conv_copies = exchange(conv_chan, conv_here, conv_s, conv_r)
    sent += conv_copies

    row_copies = []
    for step in range(1, nctx):
        target = peer(step)
        row_copies.append(
            send(
                full_cot.at[target, mine],
                cot_rows.at[mine, me],
                rows_s.at[step],
                rows_r.at[step],
                at_ctx(target),
            )
        )
    sent += row_copies
    cot_rows[mine, me] = full_cot[me, mine]

    wait_all(grad_copies)
    signal[...] = grad_conv_chan[...].astype(F32)
    spectrum(spec_g)
    f_re, f_im = spec_f[:, :width], spec_f[:, width:]
    g_re, g_im = spec_g[:, :width], spec_g[:, width:]

    def store_product(n, total):
        grad_chan[n] = total.astype(BF16)

    inverse(f_re * g_re + f_im * g_im, f_re * g_im - f_im * g_re, store_product)
    back_copies = exchange(grad_chan, grad_here, back_s, back_r)
    sent += back_copies

    wait_all(conv_copies)
    gated_all[me] = (shorts[0].astype(F32) * conv_here[...].astype(F32)).astype(BF16)
    own_gated = gated_all.at[me]
    to_x = send(own_gated, own_gated, fwd_s.at[0], fwd_r.at[0], at_ctx(x_mate))
    all_copies = [
        send(own_gated, own_gated, all_s.at[step], all_r.at[step], at_ctx(peer(step)))
        for step in range(2, nctx, 2)
    ]
    sent += [to_x] + all_copies

    right = merge_rows(gated_all[me])

    def project(group):
        start = pl.multiple_of(group * block_rows, block_rows)
        return dot(weight[pl.ds(start, block_rows), :], right)

    core = mine % 2
    pair_copies = []
    for side in range(ntp // 2):
        partial[side] = project(2 * side + 1 - core).astype(BF16)
        pair_copies.append(
            send(
                partial.at[side],
                pair_in.at[side],
                pair_s.at[side],
                pair_r.at[side],
                at_tp(core_mate),
            )
        )
    sent += pair_copies

    wait_all(row_copies)
    own_quarter = cot_rows.at[mine]
    quarter_side = send(own_quarter, own_quarter, quart_s.at[0], quart_r.at[0], at_tp(side_mate))
    quarter_core = send(own_quarter, own_quarter, quart_s.at[1], quart_r.at[1], at_tp(core_mate))
    sent += [quarter_side, quarter_core]

    wait_all(back_copies)

    def gradients(m, carry):
        back = grad_here[m].astype(F32)
        shorts_grad[0, m] = (grad_gated[m] * conv_here[m].astype(F32)).astype(BF16)
        shorts_grad[1, m] = (back * shorts[2, m].astype(F32)).astype(BF16)
        shorts_grad[2, m] = (back * shorts[1, m].astype(F32)).astype(BF16)
        return carry

    lax.fori_loop(0, nctx, gradients, 0)
    pack_edges(starts, [shorts_grad.at[index] for index in range(3)])
    halo = send(halo_out, halo_in, halo_s.at[1], halo_r.at[1], at_ctx(peer(nctx - 1)))

    my_side = mine // 2
    wait_all(pair_copies)
    pair_sum[...] = (project(side_mate) + pair_in[1 - my_side].astype(F32)).astype(BF16)
    final = send(pair_sum, final_in, final_s, final_r, at_tp(side_mate))
    sent.append(final)

    def pass_on(copy, step):
        copy.wait_recv()
        block = gated_all.at[peer(nctx - step)]
        slot = step // 2
        return send(block, block, fwd_s.at[slot], fwd_r.at[slot], at_ctx(x_mate))

    steps = list(range(2, nctx, 2))
    passed_all = [pass_on(all_copies[0], steps[0])]

    halo.wait()
    unpack_edges(starts)
    has_after = me < nctx - 1
    for index, result in enumerate((grad_query, grad_key, grad_value)):

        def long(m, carry, index=index, result=result):
            tap = taps[index, m]
            here = shorts_grad[index, m].astype(F32)
            after = jnp.where(has_after, edge[index, m], 0.0)
            total = tap[:, 0:1] * here
            for j in range(1, tap_count):
                moved = pltpu.roll(jnp.where(lane < j, after, here), width - j, 1)
                total = total + tap[:, j : j + 1] * moved
            result[m] = total.astype(BF16)
            return carry

        lax.fori_loop(0, nctx, long, 0)

    for copy, step in zip(all_copies[1:], steps[1:]):
        passed_all.append(pass_on(copy, step))
    sent += passed_all
    quarter_side.wait_recv()
    far_quarter = cot_rows.at[side_mate]
    quarter_far = send(far_quarter, far_quarter, quart_s.at[2], quart_r.at[2], at_tp(core_mate))
    sent.append(quarter_far)

    p_re, p_im = spec_p[:, :width], spec_p[:, width:]
    g_re, g_im = spec_g[:, :width], spec_g[:, width:]

    def store_filters(n, total):
        grad_filters[:, pl.ds(pl.multiple_of(n * width, width), width)] = total

    inverse(p_re * g_re + p_im * g_im, p_re * g_im - p_im * g_re, store_filters)

    own_sum = project(mine) + pair_in[my_side].astype(F32)
    final.wait_recv()
    mixed_out[...] = (own_sum + final_in[...].astype(F32)).astype(BF16)

    quarter_core.wait_recv()
    quarter_far.wait_recv()
    quarter = cot_rows.shape[2]

    def weigh(n):
        return lax.dot_general(
            cot_rows[:, n].reshape(ntp * quarter, width),
            merge_rows(gated_all[n]),
            (((1,), (1,)), ((), ())),
            preferred_element_type=F32,
        )

    grad_weight[...] = weigh(me)
    for step in steps:
        grad_weight[...] += weigh(peer(nctx - step))
    to_x.wait_recv()
    grad_weight[...] += weigh(x_mate)
    for copy, step in zip(passed_all, steps):
        copy.wait_recv()
        grad_weight[...] += weigh(lax.rem(x_mate + nctx - step, nctx))

    for copy in sent:
        copy.wait_send()


def hand_on(*refs):
    count = len(refs) // 2
    sources, dests, sem = refs[:count], refs[count:-1], refs[-1]
    copies = [
        pltpu.make_async_copy(source, dest, sem.at[index])
        for index, (source, dest) in enumerate(zip(sources, dests))
    ]
    for copy in copies:
        copy.start()
    for copy in copies:
        copy.wait()


def per_device(nctx, ntp, query_in, key_in, value_in, short_weights, filters, out_weight, cotangent):
    rows, width = query_in.shape
    channels = rows // nctx
    features = out_weight.shape[0]
    quarter = features // (nctx * ntp)
    share = nctx // ntp
    kept = nctx + 1
    outer, twists, *inner = make_tables(nctx, width)
    tap_count = short_weights.shape[2]
    tap_slots = -(-tap_count // 8) * 8
    edge_rows = -(-3 * tap_slots // 16) * 16
    ends = np.zeros((3, edge_rows, width), np.float32)
    starts = np.zeros((3, edge_rows, width), np.float32)
    for index in range(3):
        for j in range(tap_count - 1):
            ends[index, index * tap_slots + j, width - (tap_count - 1) + j] = 1.0
            starts[index, index * tap_slots + j, j] = 1.0
    blocks = (nctx, channels, width)

    def bf(*shape):
        return pltpu.VMEM(shape, BF16)

    def f32(*shape):
        return pltpu.VMEM(shape, F32)

    def sems(*shape):
        return pltpu.SemaphoreType.DMA(shape)

    vmem = pl.BlockSpec(memory_space=pltpu.VMEM)
    smem = pl.BlockSpec(memory_space=pltpu.SMEM)
    anywhere = pl.BlockSpec(memory_space=pl.ANY)
    out_shape = (
        jax.ShapeDtypeStruct((features // ntp, width), BF16),
        jax.ShapeDtypeStruct(blocks, BF16),
        jax.ShapeDtypeStruct(blocks, BF16),
        jax.ShapeDtypeStruct(blocks, BF16),
        jax.ShapeDtypeStruct((channels, nctx * width), F32),
        jax.ShapeDtypeStruct((features // nctx, rows), F32),
    )
    outs = pl.pallas_call(
        functools.partial(kernel, nctx, ntp),
        out_shape=out_shape,
        in_specs=[smem] + [vmem] * 5 + [anywhere] + [vmem] * 8,
        out_specs=tuple([vmem] * 6),
        scratch_shapes=[
            bf(features, rows),
            bf(nctx, ntp, quarter, width),
            bf(ntp, nctx, quarter, width),
            f32(3, nctx, channels, tap_slots),
            bf(edge_rows, rows),
            bf(edge_rows, rows),
            f32(3, *blocks),
            bf(3, *blocks),
            f32(*blocks),
            f32(kept * channels, 2 * width),
            f32(2, kept, channels, width),
            f32(kept * channels, 2 * width),
            f32(kept * channels, 2 * width),
            f32(kept * channels, 2 * width),
            bf(*blocks),
            bf(*blocks),
            bf(*blocks),
            bf(*blocks),
            bf(nctx, *blocks),
            f32(*blocks),
            bf(*blocks),
            bf(*blocks),
            bf(*blocks),
            bf(*blocks),
            bf(3, *blocks),
            bf(ntp // 2, features // ntp, width),
            bf(ntp // 2, features // ntp, width),
            bf(features // ntp, width),
            bf(features // ntp, width),
            pltpu.SemaphoreType.DMA,
            sems(2),
            sems(2),
            sems(3),
            sems(3),
            sems(nctx),
            sems(nctx),
            sems(3),
            sems(3),
            sems(nctx),
            sems(nctx),
            sems(nctx),
            sems(nctx),
            sems(nctx),
            sems(nctx),
            sems(nctx),
            sems(nctx),
            sems(nctx),
            sems(nctx),
            sems(nctx),
            sems(nctx),
            sems(ntp // 2),
            sems(ntp // 2),
            pltpu.SemaphoreType.DMA,
            pltpu.SemaphoreType.DMA,
        ],
        compiler_params=pltpu.CompilerParams(
            collective_id=0, has_side_effects=True, vmem_limit_bytes=56 * 1024 * 1024
        ),
        cost_estimate=pl.CostEstimate(
            flops=6 * features * rows * width, bytes_accessed=10 * features * rows // 4, transcendentals=0
        ),
        name="mixer",
    )(
        jnp.asarray(outer),
        query_in.reshape(blocks),
        key_in.reshape(blocks),
        value_in.reshape(blocks),
        short_weights.transpose(0, 2, 1),
        filters.reshape(channels, nctx * width),
        out_weight,
        cotangent.reshape(share, ntp, quarter, width),
        jnp.asarray(ends.astype(jnp.bfloat16)),
        jnp.asarray(starts.astype(jnp.bfloat16)),
        jnp.asarray(twists),
        *[jnp.asarray(table) for table in inner],
    )
    outs = pl.pallas_call(
        hand_on,
        out_shape=out_shape,
        in_specs=[anywhere] * 6,
        out_specs=tuple([anywhere] * 6),
        scratch_shapes=[sems(6)],
        name="hand_on",
    )(*outs)
    mixed, grad_query, grad_key, grad_value, grad_filters, grad_weight = outs
    return (
        mixed,
        grad_query.reshape(rows, width),
        grad_key.reshape(rows, width),
        grad_value.reshape(rows, width),
        grad_filters.reshape(filters.shape),
        grad_weight,
    )


def solution(mesh):
    placed = (
        P("tp", "ctx"),
        P("tp", "ctx"),
        P("tp", "ctx"),
        P(None, "tp", None),
        P("tp", "ctx", None),
        P(None, "tp"),
        P("tp", "ctx"),
    )
    return jax.shard_map(
        functools.partial(per_device, mesh.shape["ctx"], mesh.shape["tp"]),
        mesh=mesh,
        in_specs=placed,
        out_specs=(
            P("tp", "ctx"),
            P("tp", "ctx"),
            P("tp", "ctx"),
            P("tp", "ctx"),
            P("tp", "ctx", None),
            P("ctx", "tp"),
        ),
        check_vma=False,
    )
```

time: 74.7 us -> 121 us (1.62)
  Pallas kernels: 61.4 us -> 119 us
  local copies, waits for them, and re-layouts: 12.3 us -> 0 us
    pallas_call x1 -> x2, Pallas kernels: 61.4 us -> 119 us  [the longest x1 60.7 us: per_device(): pl.pallas_call(hand_on, out_shape=out_shape, in_specs=[anywhere] * 6, out...]
    unnamed x7 -> x0, local copies, waits for them, and re-layouts: 12.3 us -> none
where the time goes in v2:
time: 121 us; the launch traced here: 120 us
  Pallas kernels  119 us (98%)
    pallas_call x1, Pallas kernels, per_device(): pl.pallas_call(hand_on, out_shape=out_shape, in_specs=[anywhere] * 6, out...  60.7 us
    pallas_call x1, Pallas kernels, per_device(): pl.pallas_call(functools.partial(kernel, nctx, ntp), out_shape=out_shape,...  58.7 us

profile of v2, /device:TPU:0, one launch (start us, length us, event | category | flops | bytes accessed | tf_op | source)
XLA Modules:
  0.0 120.0 jit_solution(13197852609389534502)
XLA Ops:
  0.6 58.7 %mixer.1 = (bf16[1024,128]{1,0:T(8,128)(2,1)}, bf16[8,64,128]{2,1,0:T(8,128)(2,1)}, bf16[8,64,128]{2,1,0:T(8,128)(2,1)}, bf16[8,64,128]{2,1,0:T(8,128)(2,1)}, f32[64,1024]{1,0:T(8,128)}, /*index=5*/f32[512,512]{1,0:T(8,128)}) custom-call(f32[2,9,8]{2,1,0:T(8,128)} %constant.16.clone.outer, bf16[8,64,128]{2,1,0:T(8,128)(2,1)} %bitcast.13, ...), custom_call_target="tpu_custom_call" | custom-call | flops 1610612736 | bytes 5242880 | tf_op jit(solution)/shard_map/mixer/pallas_call | solution.py:556
  59.3 60.7 %hand_on.1 = (bf16[1024,128]{1,0:T(8,128)(2,1)}, bf16[8,64,128]{2,1,0:T(8,128)(2,1)}, bf16[8,64,128]{2,1,0:T(8,128)(2,1)}, bf16[8,64,128]{2,1,0:T(8,128)(2,1)}, f32[64,1024]{1,0:T(8,128)}, /*index=5*/f32[512,512]{1,0:T(8,128)}) custom-call(bf16[1024,128]{1,0:T(8,128)(2,1)} %get-tuple-element.18.refs_0_, bf16[8,64,128]{2,1,0:T(8,128)(2,1)} %get-tuple-element.19.refs_1_, ...), custom_call_target="tpu_custom_call" | custom-call | tf_op jit(solution)/shard_map/hand_on/pallas_call | solution.py:638

commit v3 on v2

--- a/solution.py
+++ b/solution.py
@@ -375,13 +375,63 @@
 
     wait_all(conv_copies)
     gated_all[me] = (shorts[0].astype(F32) * conv_here[...].astype(F32)).astype(BF16)
-    own_gated = gated_all.at[me]
-    to_x = send(own_gated, own_gated, fwd_s.at[0], fwd_r.at[0], at_ctx(x_mate))
-    all_copies = [
-        send(own_gated, own_gated, all_s.at[step], all_r.at[step], at_ctx(peer(step)))
-        for step in range(2, nctx, 2)
-    ]
-    sent += [to_x] + all_copies
+    line = nctx // 2
+    place = me // 2
+
+    def relay(step, way, action):
+        sign = 1 - 2 * way
+        block = gated_all.at[me - sign * 2 * step]
+        return pltpu.make_async_remote_copy(
+            src_ref=block,
+            dst_ref=block,
+            send_sem=all_s.at[way, step],
+            recv_sem=all_r.at[way, step + 1 - action],
+            device_id=at_ctx(me + sign * (2 - 4 * action)),
+            device_id_type=MESH,
+        )
+
+    def came(step, way):
+        return place >= step if way == 0 else place < line - step
+
+    def goes(step, way):
+        more = place < line - 1 if way == 0 else place > 0
+        return more if step == 0 else jnp.logical_and(came(step, way), more)
+
+    def to_mate(spot):
+        block = gated_all.at[2 * spot + me % 2]
+        return pltpu.make_async_remote_copy(
+            src_ref=block,
+            dst_ref=block,
+            send_sem=fwd_s.at[spot],
+            recv_sem=fwd_r.at[spot],
+            device_id=at_ctx(x_mate),
+            device_id_type=MESH,
+        )
+
+    def pass_on(step):
+        for way in range(2):
+            if step:
+
+                @pl.when(came(step, way))
+                def _():
+                    relay(step, way, 1).wait_recv()
+
+            if step < line - 1:
+
+                @pl.when(goes(step, way))
+                def _():
+                    relay(step, way, 0).start()
+
+            if step:
+
+                @pl.when(came(step, way))
+                def _():
+                    to_mate(place - step * (1 - 2 * way)).start()
+
+        if step == 0:
+            to_mate(place).start()
+
+    pass_on(0)
 
     right = merge_rows(gated_all[me])
 
@@ -429,14 +479,8 @@
     final = send(pair_sum, final_in, final_s, final_r, at_tp(side_mate))
     sent.append(final)
 
-    def pass_on(copy, step):
-        copy.wait_recv()
-        block = gated_all.at[peer(nctx - step)]
-        slot = step // 2
-        return send(block, block, fwd_s.at[slot], fwd_r.at[slot], at_ctx(x_mate))
-
-    steps = list(range(2, nctx, 2))
-    passed_all = [pass_on(all_copies[0], steps[0])]
+    for step in range(1, line - 1):
+        pass_on(step)
 
     halo.wait()
     unpack_edges(starts)
@@ -456,9 +500,7 @@
 
         lax.fori_loop(0, nctx, long, 0)
 
-    for copy, step in zip(all_copies[1:], steps[1:]):
-        passed_all.append(pass_on(copy, step))
-    sent += passed_all
+    pass_on(line - 1)
     quarter_side.wait_recv()
     far_quarter = cot_rows.at[side_mate]
     quarter_far = send(far_quarter, far_quarter, quart_s.at[2], quart_r.at[2], at_tp(core_mate))
@@ -480,38 +522,39 @@
     quarter_far.wait_recv()
     quarter = cot_rows.shape[2]
 
-    def weigh(n):
+    def weigh(column):
+        left = [
+            cot_rows[:, 2 * spot + column].reshape(ntp * quarter, width) for spot in range(line)
+        ]
+        right = [merge_rows(gated_all[2 * spot + column]) for spot in range(line)]
         return lax.dot_general(
-            cot_rows[:, n].reshape(ntp * quarter, width),
-            merge_rows(gated_all[n]),
+            jnp.concatenate(left, axis=1),
+            jnp.concatenate(right, axis=1),
             (((1,), (1,)), ((), ())),
             preferred_element_type=F32,
         )
 
-    grad_weight[...] = weigh(me)
-    for step in steps:
-        grad_weight[...] += weigh(peer(nctx - step))
-    to_x.wait_recv()
-    grad_weight[...] += weigh(x_mate)
-    for copy, step in zip(passed_all, steps):
-        copy.wait_recv()
-        grad_weight[...] += weigh(lax.rem(x_mate + nctx - step, nctx))
+    grad_weight[...] = weigh(me % 2)
+    for spot in range(line):
+        to_mate(spot).wait_recv()
+    grad_weight[...] += weigh(x_mate % 2)
 
     for copy in sent:
         copy.wait_send()
+    for spot in range(line):
+        to_mate(spot).wait_send()
+    for step in range(line - 1):
+        for way in range(2):
+
+            @pl.when(goes(step, way))
+            def _(step=step, way=way):
+                relay(step, way, 0).wait_send()
 
 
 def hand_on(*refs):
     count = len(refs) // 2
-    sources, dests, sem = refs[:count], refs[count:-1], refs[-1]
-    copies = [
-        pltpu.make_async_copy(source, dest, sem.at[index])
-        for index, (source, dest) in enumerate(zip(sources, dests))
-    ]
-    for copy in copies:
-        copy.start()
-    for copy in copies:
-        copy.wait()
+    for source, dest in zip(refs[:count], refs[count:]):
+        dest[...] = source[...]
 
 
 def per_device(nctx, ntp, query_in, key_in, value_in, short_weights, filters, out_weight, cotangent):
@@ -605,8 +648,8 @@
             sems(nctx),
             sems(nctx),
             sems(nctx),
-            sems(nctx),
-            sems(nctx),
+            sems(2, nctx // 2),
+            sems(2, nctx // 2),
             sems(nctx),
             sems(nctx),
             sems(ntp // 2),
@@ -638,9 +681,9 @@
     outs = pl.pallas_call(
         hand_on,
         out_shape=out_shape,
-        in_specs=[anywhere] * 6,
-        out_specs=tuple([anywhere] * 6),
-        scratch_shapes=[sems(6)],
+        in_specs=[vmem] * 6,
+        out_specs=tuple([vmem] * 6),
+        compiler_params=pltpu.CompilerParams(vmem_limit_bytes=16 * 1024 * 1024),
         name="hand_on",
     )(*outs)
     mixed, grad_query, grad_key, grad_value, grad_filters, grad_weight = outs

time: 121 us -> 59.7 us (0.49)
  Pallas kernels: 119 us -> 53 us
  local copies, waits for them, and re-layouts: 0 us -> 5.83 us
    pallas_call x1, Pallas kernels: 60.7 us -> 1.4 us  [per_device(): pl.pallas_call(hand_on, out_shape=out_shape, in_specs=[vmem] * 6, out_spe...]
    pallas_call x1, Pallas kernels: 58.7 us -> 51.6 us  [per_device(): pl.pallas_call(functools.partial(kernel, nctx, ntp), out_shape=out_shape,...]
    unnamed x0 -> x12, local copies, waits for them, and re-layouts: none -> 5.83 us
where the time goes in v3:
time: 59.7 us; the launch traced here: 59.4 us
  Pallas kernels  53 us (89%)
  local copies, waits for them, and re-layouts  5.83 us (10%)
  between operations  0.66 us (1%)
    pallas_call x1, Pallas kernels, per_device(): pl.pallas_call(functools.partial(kernel, nctx, ntp), out_shape=out_shape,...  51.6 us
    unnamed x12, local copies, waits for them, and re-layouts  5.83 us
    pallas_call x1, Pallas kernels, per_device(): pl.pallas_call(hand_on, out_shape=out_shape, in_specs=[vmem] * 6, out_spe...  1.4 us

profile of v3, /device:TPU:0, one launch (start us, length us, event | category | flops | bytes accessed | tf_op | source)
XLA Modules:
  0.0 59.4 jit_solution(12781039192147842037)
XLA Ops:
  0.6 51.6 %mixer.1 = (bf16[1024,128]{1,0:T(8,128)(2,1)}, bf16[8,64,128]{2,1,0:T(8,128)(2,1)}, bf16[8,64,128]{2,1,0:T(8,128)(2,1)}, bf16[8,64,128]{2,1,0:T(8,128)(2,1)}, f32[64,1024]{1,0:T(8,128)}, /*index=5*/f32[512,512]{1,0:T(8,128)}) custom-call(f32[2,9,8]{2,1,0:T(8,128)} %constant.16.clone.outer, bf16[8,64,128]{2,1,0:T(8,128)(2,1)} %bitcast.13, ...), custom_call_target="tpu_custom_call" | custom-call | flops 1610612736 | bytes 5242880 | tf_op jit(solution)/shard_map/mixer/pallas_call | solution.py:599
  52.2 0.0 copy-start
  52.2 1.2 %copy-done = f32[512,512]{1,0:T(8,128)S(1)} copy-done((f32[512,512]{1,0:T(8,128)S(1)}, f32[512,512]{1,0:T(8,128)}, u32[]{:S(2)}) %copy-start) | copy-done | bytes 1048600
  53.4 0.0 copy-start.1
  53.4 0.9 %copy-done.1 = bf16[1024,128]{1,0:T(8,128)(2,1)S(1)} copy-done((bf16[1024,128]{1,0:T(8,128)(2,1)S(1)}, bf16[1024,128]{1,0:T(8,128)(2,1)}, u32[]{:S(2)}) %copy-start.1) | copy-done | bytes 262168
  54.4 0.0 copy-start.2
  54.4 0.9 %copy-done.2 = f32[64,1024]{1,0:T(8,128)S(1)} copy-done((f32[64,1024]{1,0:T(8,128)S(1)}, f32[64,1024]{1,0:T(8,128)}, u32[]{:S(2)}) %copy-start.2) | copy-done | bytes 262168
  55.3 0.0 copy-start.3
  55.3 0.9 %copy-done.3 = bf16[8,64,128]{2,1,0:T(8,128)(2,1)S(1)} copy-done((bf16[8,64,128]{2,1,0:T(8,128)(2,1)S(1)}, bf16[8,64,128]{2,1,0:T(8,128)(2,1)}, u32[]{:S(2)}) %copy-start.3) | copy-done | bytes 131096
  56.2 0.0 copy-start.4
  56.2 0.9 %copy-done.4 = bf16[8,64,128]{2,1,0:T(8,128)(2,1)S(1)} copy-done((bf16[8,64,128]{2,1,0:T(8,128)(2,1)S(1)}, bf16[8,64,128]{2,1,0:T(8,128)(2,1)}, u32[]{:S(2)}) %copy-start.4) | copy-done | bytes 131096
  57.1 0.0 copy-start.5
  57.1 0.9 %copy-done.5 = bf16[8,64,128]{2,1,0:T(8,128)(2,1)S(1)} copy-done((bf16[8,64,128]{2,1,0:T(8,128)(2,1)S(1)}, bf16[8,64,128]{2,1,0:T(8,128)(2,1)}, u32[]{:S(2)}) %copy-start.5) | copy-done | bytes 131096
  58.0 1.4 %hand_on.1 = (bf16[1024,128]{1,0:T(8,128)(2,1)}, bf16[8,64,128]{2,1,0:T(8,128)(2,1)}, bf16[8,64,128]{2,1,0:T(8,128)(2,1)}, bf16[8,64,128]{2,1,0:T(8,128)(2,1)}, f32[64,1024]{1,0:T(8,128)}, /*index=5*/f32[512,512]{1,0:T(8,128)}) custom-call(bf16[1024,128]{1,0:T(8,128)(2,1)S(1)} %copy-done.1, bf16[8,64,128]{2,1,0:T(8,128)(2,1)S(1)} %copy-done.3, ...), custom_call_target="tpu_custom_call" | custom-call | tf_op jit(solution)/shard_map/hand_on/pallas_call | solution.py:681
Async XLA Ops:
  52.2 1.2 %copy-start = (f32[512,512]{1,0:T(8,128)S(1)}, f32[512,512]{1,0:T(8,128)}, u32[]{:S(2)}) copy-start(f32[512,512]{1,0:T(8,128)} %get-tuple-element.23.refs_5_) | copy-start | bytes 3145732
  53.4 0.9 %copy-start.1 = (bf16[1024,128]{1,0:T(8,128)(2,1)S(1)}, bf16[1024,128]{1,0:T(8,128)(2,1)}, u32[]{:S(2)}) copy-start(bf16[1024,128]{1,0:T(8,128)(2,1)} %get-tuple-element.18.refs_0_) | copy-start | bytes 786436
  54.4 0.9 %copy-start.2 = (f32[64,1024]{1,0:T(8,128)S(1)}, f32[64,1024]{1,0:T(8,128)}, u32[]{:S(2)}) copy-start(f32[64,1024]{1,0:T(8,128)} %get-tuple-element.22.refs_4_) | copy-start | bytes 786436
  55.3 0.9 %copy-start.3 = (bf16[8,64,128]{2,1,0:T(8,128)(2,1)S(1)}, bf16[8,64,128]{2,1,0:T(8,128)(2,1)}, u32[]{:S(2)}) copy-start(bf16[8,64,128]{2,1,0:T(8,128)(2,1)} %get-tuple-element.19.refs_1_) | copy-start | bytes 393220
  56.2 0.9 %copy-start.4 = (bf16[8,64,128]{2,1,0:T(8,128)(2,1)S(1)}, bf16[8,64,128]{2,1,0:T(8,128)(2,1)}, u32[]{:S(2)}) copy-start(bf16[8,64,128]{2,1,0:T(8,128)(2,1)} %get-tuple-element.20.refs_2_) | copy-start | bytes 393220
  57.1 0.9 %copy-start.5 = (bf16[8,64,128]{2,1,0:T(8,128)(2,1)S(1)}, bf16[8,64,128]{2,1,0:T(8,128)(2,1)}, u32[]{:S(2)}) copy-start(bf16[8,64,128]{2,1,0:T(8,128)(2,1)} %get-tuple-element.21.refs_3_) | copy-start | bytes 393220

commit v4 on v3

--- a/solution.py
+++ b/solution.py
@@ -56,85 +56,113 @@
     return value.reshape(blocks * rows, lanes)
 
 
-def kernel(
-    nctx,
-    ntp,
-    outer,
-    query,
-    key,
-    value,
-    taps_in,
-    filters,
-    weight_hbm,
-    cot,
-    ends,
-    starts,
-    twists,
-    fwd_high,
-    fwd_low,
-    bwd_high,
-    bwd_low,
-    mixed_out,
-    grad_query,
-    grad_key,
-    grad_value,
-    grad_filters,
-    grad_weight,
-    weight,
-    full_cot,
-    cot_rows,
-    taps,
-    halo_out,
-    halo_in,
-    edge,
-    shorts,
-    signal,
-    work,
-    parts,
-    spec_f,
-    spec_p,
-    spec_g,
-    product,
-    product_chan,
-    conv_chan,
-    conv_here,
-    gated_all,
-    grad_gated,
-    grad_conv,
-    grad_conv_chan,
-    grad_chan,
-    grad_here,
-    shorts_grad,
-    partial,
-    pair_in,
-    pair_sum,
-    final_in,
-    local_sem,
-    halo_s,
-    halo_r,
-    cot_s,
-    cot_r,
-    rows_s,
-    rows_r,
-    quart_s,
-    quart_r,
-    product_s,
-    product_r,
-    conv_s,
-    conv_r,
-    grad_s,
-    grad_r,
-    back_s,
-    back_r,
-    all_s,
-    all_r,
-    fwd_s,
-    fwd_r,
-    pair_s,
-    pair_r,
-    final_s,
-    final_r,
-):
+INPUTS = 14
+OUTPUTS = 6
+
+
+def kernel(nctx, ntp, outer, *refs):
+    given, refs = refs[:INPUTS], refs[INPUTS:]
+    wanted, refs = refs[:OUTPUTS], refs[OUTPUTS:]
+    held, refs = refs[:INPUTS], refs[INPUTS:]
+    made, refs = refs[:OUTPUTS], refs[OUTPUTS:]
+    in_sem, out_sem, *refs = refs
+    loads = {}
+    for index in (0, 1, 2, 7, 6, 3, 4, 9, 10, 11, 12, 13, 8, 5):
+        loads[index] = pltpu.make_async_copy(given[index], held[index], in_sem.at[index])
+        loads[index].start()
+
+    def loaded(*indices):
+        for index in indices:
+            loads[index].wait()
+
+    stores = []
+
+    def store(index, rows=None, slot=None):
+        source, dest = made[index], wanted[index]
+        if rows is not None:
+            source, dest = source.at[rows], dest.at[rows]
+        copy = pltpu.make_async_copy(source, dest, out_sem.at[index if slot is None else slot])
+        copy.start()
+        stores.append(copy)
+
+    (
+        query,
+        key,
+        value,
+        taps_in,
+        filters,
+        weight,
+        cot,
+        ends,
+        starts,
+        twists,
+        fwd_high,
+        fwd_low,
+        bwd_high,
+        bwd_low,
+    ) = held
+    (
+        mixed_out,
+        grad_query,
+        grad_key,
+        grad_value,
+        grad_filters,
+        grad_weight,
+    ) = made
+    (
+        full_cot,
+        cot_rows,
+        taps,
+        halo_out,
+        halo_in,
+        edge,
+        shorts,
+        signal,
+        work,
+        parts,
+        spec_f,
+        spec_p,
+        spec_g,
+        product,
+        product_chan,
+        conv_chan,
+        conv_here,
+        gated_all,
+        grad_gated,
+        grad_conv,
+        grad_conv_chan,
+        grad_chan,
+        grad_here,
+        shorts_grad,
+        partial,
+        pair_in,
+        pair_sum,
+        final_in,
+        halo_s,
+        halo_r,
+        cot_s,
+        cot_r,
+        rows_s,
+        rows_r,
+        quart_s,
+        quart_r,
+        product_s,
+        product_r,
+        conv_s,
+        conv_r,
+        grad_s,
+        grad_r,
+        back_s,
+        back_r,
+        all_s,
+        all_r,
+        fwd_s,
+        fwd_r,
+        pair_s,
+        pair_r,
+        final_s,
+        final_r,
+    ) = refs
     channels, width = query.shape[1:]
     kept = nctx + 1
     tap_count = taps_in.shape[1]
@@ -188,9 +216,6 @@
         for copy in copies:
             copy.wait_recv()
 
-    load_weight = pltpu.make_async_copy(weight_hbm, weight, local_sem)
-    load_weight.start()
-
     barrier = pltpu.get_barrier_semaphore()
     for step in range(1, nctx):
         pl.semaphore_signal(barrier, inc=1, device_id=at_ctx(peer(step)), device_id_type=MESH)
@@ -214,16 +239,19 @@
             )
             edge[index] = spread.reshape(nctx, channels, width)
 
+    loaded(0, 1, 2, 7)
     pack_edges(ends, (query, key, value))
     pl.semaphore_wait(barrier, nctx + 1)
 
     sent = []
     halo = send(halo_out, halo_in, halo_s.at[0], halo_r.at[0], at_ctx(peer(1)))
+    loaded(6)
     own_rows = full_cot.at[pl.ds(mine * share, share)]
     to_side = send(cot, own_rows, cot_s.at[0], cot_r.at[0], at_tp(side_mate))
     to_core = send(cot, own_rows, cot_s.at[1], cot_r.at[1], at_tp(core_mate))
     sent += [to_side, to_core]
     full_cot[pl.ds(mine * share, share)] = cot[...]
+    loaded(3)
     for index in range(3):
         padded = jnp.concatenate(
             [taps_in[index], jnp.zeros((taps.shape[3] - tap_count, nctx * channels), F32)], axis=0
@@ -275,6 +303,7 @@
 
     lane = lax.broadcasted_iota(jnp.int32, (channels, width), 1)
 
+    loaded(4, 9, 10, 11)
     for n in range(nctx):
         signal[n] = filters[:, n * width : (n + 1) * width]
     spectrum(spec_f)
@@ -310,7 +339,7 @@
     passed_rows = full_cot.at[pl.ds(side_mate * share, share)]
     passed = send(passed_rows, passed_rows, cot_s.at[2], cot_r.at[2], at_tp(core_mate))
     sent.append(passed)
-    load_weight.wait()
+    loaded(5, 8, 12, 13)
     to_core.wait_recv()
 
     def gate_part(group):
@@ -479,8 +508,7 @@
     final = send(pair_sum, final_in, final_s, final_r, at_tp(side_mate))
     sent.append(final)
 
-    for step in range(1, line - 1):
-        pass_on(step)
+    pass_on(1)
 
     halo.wait()
     unpack_edges(starts)
@@ -499,45 +527,59 @@
             return carry
 
         lax.fori_loop(0, nctx, long, 0)
-
-    pass_on(line - 1)
+        store(1 + index)
+
+    for step in range(2, line - 1):
+        pass_on(step)
+
+    p_re, p_im = spec_p[:, :width], spec_p[:, width:]
+    g_re, g_im = spec_g[:, :width], spec_g[:, width:]
+
+    def store_filters(n, total):
+        grad_filters[:, pl.ds(pl.multiple_of(n * width, width), width)] = total
+
+    inverse(p_re * g_re + p_im * g_im, p_re * g_im - p_im * g_re, store_filters)
+    store(4)
+    if line > 2:
+        pass_on(line - 1)
     quarter_side.wait_recv()
     far_quarter = cot_rows.at[side_mate]
     quarter_far = send(far_quarter, far_quarter, quart_s.at[2], quart_r.at[2], at_tp(core_mate))
     sent.append(quarter_far)
 
-    p_re, p_im = spec_p[:, :width], spec_p[:, width:]
-    g_re, g_im = spec_g[:, :width], spec_g[:, width:]
-
-    def store_filters(n, total):
-        grad_filters[:, pl.ds(pl.multiple_of(n * width, width), width)] = total
-
-    inverse(p_re * g_re + p_im * g_im, p_re * g_im - p_im * g_re, store_filters)
-
     own_sum = project(mine) + pair_in[my_side].astype(F32)
     final.wait_recv()
     mixed_out[...] = (own_sum + final_in[...].astype(F32)).astype(BF16)
+    store(0)
 
     quarter_core.wait_recv()
     quarter_far.wait_recv()
     quarter = cot_rows.shape[2]
 
-    def weigh(column):
-        left = [
-            cot_rows[:, 2 * spot + column].reshape(ntp * quarter, width) for spot in range(line)
-        ]
-        right = [merge_rows(gated_all[2 * spot + column]) for spot in range(line)]
+    def over_line(column):
+        blocks = [merge_rows(gated_all[2 * spot + column]) for spot in range(line)]
+        return jnp.concatenate(blocks, axis=1)
+
+    def weigh(group, column, right):
+        left = [cot_rows[group, 2 * spot + column] for spot in range(line)]
         return lax.dot_general(
             jnp.concatenate(left, axis=1),
-            jnp.concatenate(right, axis=1),
+            right,
             (((1,), (1,)), ((), ())),
             preferred_element_type=F32,
         )
 
-    grad_weight[...] = weigh(me % 2)
+    right = over_line(me % 2)
+    for group in range(ntp):
+        rows = slice(group * quarter, (group + 1) * quarter)
+        grad_weight[rows, :] = weigh(group, me % 2, right)
     for spot in range(line):
         to_mate(spot).wait_recv()
-    grad_weight[...] += weigh(x_mate % 2)
+    right = over_line(x_mate % 2)
+    for group in range(ntp):
+        rows = slice(group * quarter, (group + 1) * quarter)
+        grad_weight[rows, :] += weigh(group, x_mate % 2, right)
+        store(5, pl.ds(group * quarter, quarter), OUTPUTS - 1 + group)
 
     for copy in sent:
         copy.wait_send()
@@ -549,12 +591,29 @@
             @pl.when(goes(step, way))
             def _(step=step, way=way):
                 relay(step, way, 0).wait_send()
+    for copy in stores:
+        copy.wait()
 
 
 def hand_on(*refs):
-    count = len(refs) // 2
-    for source, dest in zip(refs[:count], refs[count:]):
-        dest[...] = source[...]
+    count = (len(refs) - 2) // 3
+    sources, dests, held = refs[:count], refs[count : 2 * count], refs[2 * count : 3 * count]
+    in_sem, out_sem = refs[3 * count :]
+    loads = [
+        pltpu.make_async_copy(source, place, in_sem.at[index])
+        for index, (source, place) in enumerate(zip(sources, held))
+    ]
+    stores = [
+        pltpu.make_async_copy(place, dest, out_sem.at[index])
+        for index, (place, dest) in enumerate(zip(held, dests))
+    ]
+    for load in loads:
+        load.start()
+    for load, store in zip(loads, stores):
+        load.wait()
+        store.start()
+    for store in stores:
+        store.wait()
 
 
 def per_device(nctx, ntp, query_in, key_in, value_in, short_weights, filters, out_weight, cotangent):
@@ -585,7 +644,6 @@
     def sems(*shape):
         return pltpu.SemaphoreType.DMA(shape)
 
-    vmem = pl.BlockSpec(memory_space=pltpu.VMEM)
     smem = pl.BlockSpec(memory_space=pltpu.SMEM)
     anywhere = pl.BlockSpec(memory_space=pl.ANY)
     out_shape = (
@@ -596,13 +654,29 @@
         jax.ShapeDtypeStruct((channels, nctx * width), F32),
         jax.ShapeDtypeStruct((features // nctx, rows), F32),
     )
+    arrays = (
+        query_in.reshape(blocks),
+        key_in.reshape(blocks),
+        value_in.reshape(blocks),
+        short_weights.transpose(0, 2, 1),
+        filters.reshape(channels, nctx * width),
+        out_weight,
+        cotangent.reshape(share, ntp, quarter, width),
+        jnp.asarray(ends.astype(jnp.bfloat16)),
+        jnp.asarray(starts.astype(jnp.bfloat16)),
+        jnp.asarray(twists),
+        *[jnp.asarray(table) for table in inner],
+    )
     outs = pl.pallas_call(
         functools.partial(kernel, nctx, ntp),
         out_shape=out_shape,
-        in_specs=[smem] + [vmem] * 5 + [anywhere] + [vmem] * 8,
-        out_specs=tuple([vmem] * 6),
-        scratch_shapes=[
-            bf(features, rows),
+        in_specs=[smem] + [anywhere] * INPUTS,
+        out_specs=tuple([anywhere] * OUTPUTS),
+        scratch_shapes=[pltpu.VMEM(array.shape, array.dtype) for array in arrays]
+        + [pltpu.VMEM(shape.shape, shape.dtype) for shape in out_shape]
+        + [
+            sems(INPUTS),
+            sems(OUTPUTS - 1 + ntp),
             bf(nctx, ntp, quarter, width),
             bf(ntp, nctx, quarter, width),
             f32(3, nctx, channels, tap_slots),
@@ -631,7 +705,6 @@
             bf(ntp // 2, features // ntp, width),
             bf(features // ntp, width),
             bf(features // ntp, width),
-            pltpu.SemaphoreType.DMA,
             sems(2),
             sems(2),
             sems(3),
@@ -666,24 +739,16 @@
         name="mixer",
     )(
         jnp.asarray(outer),
-        query_in.reshape(blocks),
-        key_in.reshape(blocks),
-        value_in.reshape(blocks),
-        short_weights.transpose(0, 2, 1),
-        filters.reshape(channels, nctx * width),
-        out_weight,
-        cotangent.reshape(share, ntp, quarter, width),
-        jnp.asarray(ends.astype(jnp.bfloat16)),
-        jnp.asarray(starts.astype(jnp.bfloat16)),
-        jnp.asarray(twists),
-        *[jnp.asarray(table) for table in inner],
+        *arrays,
     )
     outs = pl.pallas_call(
         hand_on,
         out_shape=out_shape,
-        in_specs=[vmem] * 6,
-        out_specs=tuple([vmem] * 6),
-        compiler_params=pltpu.CompilerParams(vmem_limit_bytes=16 * 1024 * 1024),
+        in_specs=[anywhere] * OUTPUTS,
+        out_specs=tuple([anywhere] * OUTPUTS),
+        scratch_shapes=[pltpu.VMEM(shape.shape, shape.dtype) for shape in out_shape]
+        + [sems(OUTPUTS), sems(OUTPUTS)],
+        compiler_params=pltpu.CompilerParams(vmem_limit_bytes=56 * 1024 * 1024),
         name="hand_on",
     )(*outs)
     mixed, grad_query, grad_key, grad_value, grad_filters, grad_weight = outs

time: 59.7 us -> 56.5 us (0.946)
  local copies, waits for them, and re-layouts: 5.83 us -> 0 us
  Pallas kernels: 53 us -> 55.7 us
    unnamed x12 -> x0, local copies, waits for them, and re-layouts: 5.83 us -> none
    pallas_call x1, Pallas kernels: 51.6 us -> 53 us  [per_device(): pl.pallas_call(functools.partial(kernel, nctx, ntp), out_shape=out_shape,...]
    pallas_call x1, Pallas kernels: 1.4 us -> 2.63 us  [per_device(): pl.pallas_call(hand_on, out_shape=out_shape, in_specs=[anywhere] * OUTPUT...]
where the time goes in v4:
time: 56.5 us; the launch traced here: 56.3 us
  Pallas kernels  55.7 us (99%)
  between operations  0.64 us (1%)
    pallas_call x1, Pallas kernels, per_device(): pl.pallas_call(functools.partial(kernel, nctx, ntp), out_shape=out_shape,...  53 us
    pallas_call x1, Pallas kernels, per_device(): pl.pallas_call(hand_on, out_shape=out_shape, in_specs=[anywhere] * OUTPUT...  2.63 us

profile of v4, /device:TPU:0, one launch (start us, length us, event | category | flops | bytes accessed | tf_op | source)
XLA Modules:
  0.0 56.3 jit_solution(1152473255577842086)
XLA Ops:
  0.6 53.0 %mixer.1 = (bf16[1024,128]{1,0:T(8,128)(2,1)}, bf16[8,64,128]{2,1,0:T(8,128)(2,1)}, bf16[8,64,128]{2,1,0:T(8,128)(2,1)}, bf16[8,64,128]{2,1,0:T(8,128)(2,1)}, f32[64,1024]{1,0:T(8,128)}, /*index=5*/f32[512,512]{1,0:T(8,128)}) custom-call(f32[2,9,8]{2,1,0:T(8,128)} %constant.23.clone.outer, bf16[8,64,128]{2,1,0:T(8,128)(2,1)} %bitcast.13, ...), custom_call_target="tpu_custom_call" | custom-call | flops 1610612736 | bytes 5242880 | tf_op jit(solution)/shard_map/mixer/pallas_call | solution.py:670
  53.7 2.6 %hand_on.1 = (bf16[1024,128]{1,0:T(8,128)(2,1)}, bf16[8,64,128]{2,1,0:T(8,128)(2,1)}, bf16[8,64,128]{2,1,0:T(8,128)(2,1)}, bf16[8,64,128]{2,1,0:T(8,128)(2,1)}, f32[64,1024]{1,0:T(8,128)}, /*index=5*/f32[512,512]{1,0:T(8,128)}) custom-call(bf16[1024,128]{1,0:T(8,128)(2,1)} %get-tuple-element.18.refs_0_, bf16[8,64,128]{2,1,0:T(8,128)(2,1)} %get-tuple-element.19.refs_1_, ...), custom_call_target="tpu_custom_call" | custom-call | tf_op jit(solution)/shard_map/hand_on/pallas_call | solution.py:744

commit v5 on v4

--- a/solution.py
+++ b/solution.py
@@ -333,14 +333,54 @@
     product[...] = (shorts[1].astype(F32) * shorts[2].astype(F32)).astype(BF16)
     product_copies = exchange(product, product_chan, product_s, product_r)
     sent += product_copies
+    row_copies = [
+        pltpu.make_async_remote_copy(
+            src_ref=full_cot.at[peer(step), mine],
+            dst_ref=cot_rows.at[mine, me],
+            send_sem=rows_s.at[step],
+            recv_sem=rows_r.at[step],
+            device_id=at_ctx(peer(step)),
+            device_id_type=MESH,
+        )
+        for step in range(1, nctx)
+    ]
+    sent += row_copies
+
+    def send_rows(held_first):
+        for step, copy in zip(range(1, nctx), row_copies):
+            first = (peer(step) // share) // 2 == mine // 2
+
+            @pl.when(first if held_first else jnp.logical_not(first))
+            def _(copy=copy):
+                copy.start()
+
+    to_core.wait_recv()
+    send_rows(True)
     short(0)
 
     to_side.wait_recv()
     passed_rows = full_cot.at[pl.ds(side_mate * share, share)]
     passed = send(passed_rows, passed_rows, cot_s.at[2], cot_r.at[2], at_tp(core_mate))
     sent.append(passed)
+
+    wait_all(product_copies)
     loaded(5, 8, 12, 13)
-    to_core.wait_recv()
+    signal[...] = product_chan[...].astype(F32)
+    spectrum(spec_p)
+    passed.wait_recv()
+    send_rows(False)
+    cot_rows[mine, me] = full_cot[me, mine]
+
+    f_re, f_im = spec_f[:, :width], spec_f[:, width:]
+    p_re, p_im = spec_p[:, :width], spec_p[:, width:]
+
+    def store_convolved(n, total):
+        conv_chan[n] = total.astype(BF16)
+
+    inverse(p_re * f_re - p_im * f_im, p_re * f_im + p_im * f_re, store_convolved)
+    conv_copies = exchange(conv_chan, conv_here, conv_s, conv_r)
+    sent += conv_copies
+
 
     def gate_part(group):
         cot_block = full_cot[pl.ds(group * share, share)].reshape(block_rows, width)
@@ -353,54 +393,11 @@
         )
 
     total = gate_part(mine) + gate_part(core_mate) + gate_part(side_mate)
-    passed.wait_recv()
     total = total + gate_part(far_mate)
     grad_gated[...] = total.T.reshape(nctx, channels, width)
     grad_conv[...] = (grad_gated[...] * shorts[0].astype(F32)).astype(BF16)
     grad_copies = exchange(grad_conv, grad_conv_chan, grad_s, grad_r)
     sent += grad_copies
-
-    wait_all(product_copies)
-    signal[...] = product_chan[...].astype(F32)
-    spectrum(spec_p)
-
-    f_re, f_im = spec_f[:, :width], spec_f[:, width:]
-    p_re, p_im = spec_p[:, :width], spec_p[:, width:]
-
-    def store_convolved(n, total):
-        conv_chan[n] = total.astype(BF16)
-
-    inverse(p_re * f_re - p_im * f_im, p_re * f_im + p_im * f_re, store_convolved)
-    conv_copies = exchange(conv_chan, conv_here, conv_s, conv_r)
-    sent += conv_copies
-
-    row_copies = []
-    for step in range(1, nctx):
-        target = peer(step)
-        row_copies.append(
-            send(
-                full_cot.at[target, mine],
-                cot_rows.at[mine, me],
-                rows_s.at[step],
-                rows_r.at[step],
-                at_ctx(target),
-            )
-        )
-    sent += row_copies
-    cot_rows[mine, me] = full_cot[me, mine]
-
-    wait_all(grad_copies)
-    signal[...] = grad_conv_chan[...].astype(F32)
-    spectrum(spec_g)
-    f_re, f_im = spec_f[:, :width], spec_f[:, width:]
-    g_re, g_im = spec_g[:, :width], spec_g[:, width:]
-
-    def store_product(n, total):
-        grad_chan[n] = total.astype(BF16)
-
-    inverse(f_re * g_re + f_im * g_im, f_re * g_im - f_im * g_re, store_product)
-    back_copies = exchange(grad_chan, grad_here, back_s, back_r)
-    sent += back_copies
 
     wait_all(conv_copies)
     gated_all[me] = (shorts[0].astype(F32) * conv_here[...].astype(F32)).astype(BF16)
@@ -489,6 +486,27 @@
     quarter_core = send(own_quarter, own_quarter, quart_s.at[1], quart_r.at[1], at_tp(core_mate))
     sent += [quarter_side, quarter_core]
 
+    wait_all(grad_copies)
+    signal[...] = grad_conv_chan[...].astype(F32)
+    spectrum(spec_g)
+    f_re, f_im = spec_f[:, :width], spec_f[:, width:]
+    g_re, g_im = spec_g[:, :width], spec_g[:, width:]
+
+    def store_product(n, total):
+        grad_chan[n] = total.astype(BF16)
+
+    inverse(f_re * g_re + f_im * g_im, f_re * g_im - f_im * g_re, store_product)
+    back_copies = exchange(grad_chan, grad_here, back_s, back_r)
+    sent += back_copies
+
+    pass_on(1)
+
+    my_side = mine // 2
+    wait_all(pair_copies)
+    pair_sum[...] = (project(side_mate) + pair_in[1 - my_side].astype(F32)).astype(BF16)
+    final = send(pair_sum, final_in, final_s, final_r, at_tp(side_mate))
+    sent.append(final)
+
     wait_all(back_copies)
 
     def gradients(m, carry):
@@ -502,14 +520,17 @@
     pack_edges(starts, [shorts_grad.at[index] for index in range(3)])
     halo = send(halo_out, halo_in, halo_s.at[1], halo_r.at[1], at_ctx(peer(nctx - 1)))
 
-    my_side = mine // 2
-    wait_all(pair_copies)
-    pair_sum[...] = (project(side_mate) + pair_in[1 - my_side].astype(F32)).astype(BF16)
-    final = send(pair_sum, final_in, final_s, final_r, at_tp(side_mate))
-    sent.append(final)
-
-    pass_on(1)
-
+    for step in range(2, line - 1):
+        pass_on(step)
+
+    p_re, p_im = spec_p[:, :width], spec_p[:, width:]
+    g_re, g_im = spec_g[:, :width], spec_g[:, width:]
+
+    def store_filters(n, total):
+        grad_filters[:, pl.ds(pl.multiple_of(n * width, width), width)] = total
+
+    inverse(p_re * g_re + p_im * g_im, p_re * g_im - p_im * g_re, store_filters)
+    store(4)
     halo.wait()
     unpack_edges(starts)
     has_after = me < nctx - 1
@@ -529,17 +550,6 @@
         lax.fori_loop(0, nctx, long, 0)
         store(1 + index)
 
-    for step in range(2, line - 1):
-        pass_on(step)
-
-    p_re, p_im = spec_p[:, :width], spec_p[:, width:]
-    g_re, g_im = spec_g[:, :width], spec_g[:, width:]
-
-    def store_filters(n, total):
-        grad_filters[:, pl.ds(pl.multiple_of(n * width, width), width)] = total
-
-    inverse(p_re * g_re + p_im * g_im, p_re * g_im - p_im * g_re, store_filters)
-    store(4)
     if line > 2:
         pass_on(line - 1)
     quarter_side.wait_recv()

time: 56.5 us -> 58.6 us (1.037)
  Pallas kernels: 55.7 us -> 57.7 us
    pallas_call x1, Pallas kernels: 53 us -> 55.1 us  [per_device(): pl.pallas_call(functools.partial(kernel, nctx, ntp), out_shape=out_shape,...]
where the time goes in v5:
time: 58.6 us; the launch traced here: 58.4 us
  Pallas kernels  57.7 us (98%)
  between operations  0.64 us (1%)
    pallas_call x1, Pallas kernels, per_device(): pl.pallas_call(functools.partial(kernel, nctx, ntp), out_shape=out_shape,...  55.1 us
    pallas_call x1, Pallas kernels, per_device(): pl.pallas_call(hand_on, out_shape=out_shape, in_specs=[anywhere] * OUTPUT...  2.63 us

profile of v5, /device:TPU:0, one launch (start us, length us, event | category | flops | bytes accessed | tf_op | source)
XLA Modules:
  0.0 58.4 jit_solution(17203188871850290089)
XLA Ops:
  0.6 55.1 %mixer.1 = (bf16[1024,128]{1,0:T(8,128)(2,1)}, bf16[8,64,128]{2,1,0:T(8,128)(2,1)}, bf16[8,64,128]{2,1,0:T(8,128)(2,1)}, bf16[8,64,128]{2,1,0:T(8,128)(2,1)}, f32[64,1024]{1,0:T(8,128)}, /*index=5*/f32[512,512]{1,0:T(8,128)}) custom-call(f32[2,9,8]{2,1,0:T(8,128)} %constant.23.clone.outer, bf16[8,64,128]{2,1,0:T(8,128)(2,1)} %bitcast.13, ...), custom_call_target="tpu_custom_call" | custom-call | flops 1610612736 | bytes 5242880 | tf_op jit(solution)/shard_map/mixer/pallas_call | solution.py:680
  55.8 2.6 %hand_on.1 = (bf16[1024,128]{1,0:T(8,128)(2,1)}, bf16[8,64,128]{2,1,0:T(8,128)(2,1)}, bf16[8,64,128]{2,1,0:T(8,128)(2,1)}, bf16[8,64,128]{2,1,0:T(8,128)(2,1)}, f32[64,1024]{1,0:T(8,128)}, /*index=5*/f32[512,512]{1,0:T(8,128)}) custom-call(bf16[1024,128]{1,0:T(8,128)(2,1)} %get-tuple-element.18.refs_0_, bf16[8,64,128]{2,1,0:T(8,128)(2,1)} %get-tuple-element.19.refs_1_, ...), custom_call_target="tpu_custom_call" | custom-call | tf_op jit(solution)/shard_map/hand_on/pallas_call | solution.py:754

commit v6 on v4

--- a/solution.py
+++ b/solution.py
@@ -25,7 +25,7 @@
     full = rows * width
     kept = blocks + 1
     turn = np.outer(np.arange(kept), np.arange(blocks)) % rows * (2 * np.pi / rows)
-    outer = np.stack([np.cos(turn), -np.sin(turn)]).astype(np.float32)
+    outer = np.stack([np.cos(turn), -np.sin(turn)])
     twist = np.outer(np.arange(kept), np.arange(width)) % full * (2 * np.pi / full)
     weight = np.full((kept, 1), 2.0 / full)
     weight[0] = weight[-1] = 1.0 / full
@@ -47,6 +47,32 @@
     value_high = value.astype(BF16)
     value_low = (value - value_high.astype(F32)).astype(BF16)
     return dot(value_high, high) + dot(value_low, high) + dot(value_high, low)
+
+
+def repeat(count, body):
+    if count <= 16:
+        for index in range(count):
+            body(index, 0)
+    else:
+        lax.fori_loop(0, count, body, 0)
+
+
+def window(index, size):
+    if isinstance(index, int):
+        return pl.ds(index * size, size)
+    return pl.ds(pl.multiple_of(index * size, size), size)
+
+
+def add_term(total, factor, block):
+    if isinstance(factor, float):
+        if abs(factor) < 1e-9:
+            return total
+        if abs(abs(factor) - 1.0) < 1e-9:
+            if total is None:
+                return block if factor > 0 else -block
+            return total + block if factor > 0 else total - block
+    term = factor * block
+    return term if total is None else total + term
 
 
 def merge_rows(value):
@@ -258,21 +284,29 @@
         )
         taps[index] = padded.T.reshape(nctx, channels, taps.shape[3])
 
+    table = make_tables(nctx, width)[0]
+
+    def factor(part, k, n):
+        if isinstance(k, int) and isinstance(n, int):
+            return float(table[part, k, n])
+        return outer[part, k, n]
+
     def spectrum(spec):
         def one(k, carry):
-            re = jnp.zeros((channels, width), F32)
-            im = jnp.zeros((channels, width), F32)
+            re = im = None
             for n in range(nctx):
                 block = signal[n]
-                re = re + outer[0, k, n] * block
-                im = im + outer[1, k, n] * block
+                re = add_term(re, factor(0, k, n), block)
+                im = add_term(im, factor(1, k, n), block)
+            if im is None:
+                im = jnp.zeros((channels, width), F32)
             cos, sin = twists[0, k], twists[1, k]
-            rows = pl.ds(pl.multiple_of(k * channels, channels), channels)
+            rows = window(k, channels)
             work[rows, :width] = re * cos - im * sin
             work[rows, width:] = re * sin + im * cos
             return carry
 
-        lax.fori_loop(0, kept, one, 0)
+        repeat(kept, one)
         spec[...] = dot_split(work[...], fwd_high[...], fwd_low[...])
 
     def inverse(re, im, store):
@@ -281,25 +315,25 @@
         work[...] = dot_split(work[...], bwd_high[...], bwd_low[...])
 
         def turn(k, carry):
-            rows = pl.ds(pl.multiple_of(k * channels, channels), channels)
+            rows = window(k, channels)
             back_re, back_im = work[rows, :width], work[rows, width:]
             cos, sin = twists[2, k], twists[3, k]
             parts[0, k] = back_re * cos + back_im * sin
             parts[1, k] = back_im * cos - back_re * sin
             return carry
 
-        lax.fori_loop(0, kept, turn, 0)
+        repeat(kept, turn)
 
         def one(n, carry):
             total = parts[0, 0]
             for k in range(1, kept):
-                total = total + outer[0, k, n] * parts[0, k]
+                total = add_term(total, factor(0, k, n), parts[0, k])
                 if k < nctx:
-                    total = total + outer[1, k, n] * parts[1, k]
+                    total = add_term(total, factor(1, k, n), parts[1, k])
             store(n, total)
             return carry
 
-        lax.fori_loop(0, nctx, one, 0)
+        repeat(nctx, one)
 
     lane = lax.broadcasted_iota(jnp.int32, (channels, width), 1)
 
@@ -326,7 +360,7 @@
             shorts[index, m] = total.astype(BF16)
             return carry
 
-        lax.fori_loop(0, nctx, one, 0)
+        repeat(nctx, one)
 
     short(1)
     short(2)
@@ -498,7 +532,7 @@
         shorts_grad[2, m] = (back * shorts[1, m].astype(F32)).astype(BF16)
         return carry
 
-    lax.fori_loop(0, nctx, gradients, 0)
+    repeat(nctx, gradients)
     pack_edges(starts, [shorts_grad.at[index] for index in range(3)])
     halo = send(halo_out, halo_in, halo_s.at[1], halo_r.at[1], at_ctx(peer(nctx - 1)))
 
@@ -526,7 +560,7 @@
             result[m] = total.astype(BF16)
             return carry
 
-        lax.fori_loop(0, nctx, long, 0)
+        repeat(nctx, long)
         store(1 + index)
 
     for step in range(2, line - 1):
@@ -536,7 +570,7 @@
     g_re, g_im = spec_g[:, :width], spec_g[:, width:]
 
     def store_filters(n, total):
-        grad_filters[:, pl.ds(pl.multiple_of(n * width, width), width)] = total
+        grad_filters[:, window(n, width)] = total
 
     inverse(p_re * g_re + p_im * g_im, p_re * g_im - p_im * g_re, store_filters)
     store(4)
@@ -738,7 +772,7 @@
         ),
         name="mixer",
     )(
-        jnp.asarray(outer),
+        jnp.asarray(outer.astype(np.float32)),
         *arrays,
     )
     outs = pl.pallas_call(

time: 56.5 us -> 54.4 us (0.963)
  Pallas kernels: 55.7 us -> 53.5 us
    pallas_call x1, Pallas kernels: 53 us -> 50.9 us  [per_device(): pl.pallas_call(functools.partial(kernel, nctx, ntp), out_shape=out_shape,...]
where the time goes in v6:
time: 54.4 us; the launch traced here: 54.1 us
  Pallas kernels  53.5 us (98%)
  between operations  0.64 us (1%)
    pallas_call x1, Pallas kernels, per_device(): pl.pallas_call(functools.partial(kernel, nctx, ntp), out_shape=out_shape,...  50.9 us
    pallas_call x1, Pallas kernels, per_device(): pl.pallas_call(hand_on, out_shape=out_shape, in_specs=[anywhere] * OUTPUT...  2.63 us

profile of v6, /device:TPU:0, one launch (start us, length us, event | category | flops | bytes accessed | tf_op | source)
XLA Modules:
  0.0 54.1 jit_solution(9172584655015898696)
XLA Ops:
  0.6 50.9 %mixer.1 = (bf16[1024,128]{1,0:T(8,128)(2,1)}, bf16[8,64,128]{2,1,0:T(8,128)(2,1)}, bf16[8,64,128]{2,1,0:T(8,128)(2,1)}, bf16[8,64,128]{2,1,0:T(8,128)(2,1)}, f32[64,1024]{1,0:T(8,128)}, /*index=5*/f32[512,512]{1,0:T(8,128)}) custom-call(f32[2,9,8]{2,1,0:T(8,128)} %constant.23.clone.outer, bf16[8,64,128]{2,1,0:T(8,128)(2,1)} %bitcast.13, ...), custom_call_target="tpu_custom_call" | custom-call | flops 1610612736 | bytes 5242880 | tf_op jit(solution)/shard_map/mixer/pallas_call | solution.py:704
  51.5 2.6 %hand_on.1 = (bf16[1024,128]{1,0:T(8,128)(2,1)}, bf16[8,64,128]{2,1,0:T(8,128)(2,1)}, bf16[8,64,128]{2,1,0:T(8,128)(2,1)}, bf16[8,64,128]{2,1,0:T(8,128)(2,1)}, f32[64,1024]{1,0:T(8,128)}, /*index=5*/f32[512,512]{1,0:T(8,128)}) custom-call(bf16[1024,128]{1,0:T(8,128)(2,1)} %get-tuple-element.18.refs_0_, bf16[8,64,128]{2,1,0:T(8,128)(2,1)} %get-tuple-element.19.refs_1_, ...), custom_call_target="tpu_custom_call" | custom-call | tf_op jit(solution)/shard_map/hand_on/pallas_call | solution.py:778
